TPU v7x, 32 devices: a whole 2x2x4 slice. The times are simulated.
32 devices in a mesh: seq: 8 (over z, x), batch: 4 (over y, core).
Axes of the slice: x: 2, y: 2, z: 4, core: 2. Of those that a mesh axis runs over, the one named last changes fastest.
Arguments:
- inputs: bfloat16 [2, 4, 2048, 768], P(None, 'batch', 'seq'), may hold values from -6 to 6
- cotangent: bfloat16 [2, 4, 2048, 768], P(None, 'batch', 'seq'), may hold values from -6 to 6
- doc_lengths: int32 [2, 4, 4], P(None, 'batch'), may hold values from 0 to 2048, as said below
- random_blocks: int32 [2, 4, 32, 3], P(None, 'batch'), may hold values from 0 to 31, as said below
- w_query: bfloat16 [768, 768], P(('seq', 'batch')), may hold values from -0.21875 to 0.21875
- w_key: bfloat16 [768, 768], P(('seq', 'batch')), may hold values from -0.21875 to 0.21875
- w_value: bfloat16 [768, 768], P(('seq', 'batch')), may hold values from -0.21875 to 0.21875
- w_out: bfloat16 [768, 768], P(('seq', 'batch')), may hold values from -0.875 to 0.875
- w_up: bfloat16 [768, 3072], P(('seq', 'batch')), may hold values from -0.21875 to 0.21875
- w_down: bfloat16 [3072, 768], P(('seq', 'batch')), may hold values from -0.109375 to 0.109375
- b_query: bfloat16 [768], P(('seq', 'batch')), may hold values from -3 to 3
- b_value: bfloat16 [768], P(('seq', 'batch')), may hold values from -3 to 3
- b_out: bfloat16 [768], P(('seq', 'batch')), may hold values from -3 to 3
- b_up: bfloat16 [3072], P(('seq', 'batch')), may hold values from -3 to 3
- b_down: bfloat16 [768], P(('seq', 'batch')), may hold values from -3 to 3
- gain_attn: bfloat16 [768], P(('seq', 'batch')), may hold values from 0.5 to 1.5
- bias_attn: bfloat16 [768], P(('seq', 'batch')), may hold values from -3 to 3
- gain_ffn: bfloat16 [768], P(('seq', 'batch')), may hold values from 0.5 to 1.5
- bias_ffn: bfloat16 [768], P(('seq', 'batch')), may hold values from -3 to 3
Outputs:
- outputs: bfloat16 [2, 4, 2048, 768], P(None, 'batch', 'seq')
- grad_inputs: float32 [2, 4, 2048, 768], P(None, 'batch', 'seq')
- grad_w_query: float32 [768, 768], P(('seq', 'batch'))
- grad_w_key: float32 [768, 768], P(('seq', 'batch'))
- grad_w_value: float32 [768, 768], P(('seq', 'batch'))
- grad_w_out: float32 [768, 768], P(('seq', 'batch'))
- grad_w_up: float32 [768, 3072], P(('seq', 'batch'))
- grad_w_down: float32 [3072, 768], P(('seq', 'batch'))
- grad_b_query: float32 [768], P(('seq', 'batch'))
- grad_b_value: float32 [768], P(('seq', 'batch'))
- grad_b_out: float32 [768], P(('seq', 'batch'))
- grad_b_up: float32 [3072], P(('seq', 'batch'))
- grad_b_down: float32 [768], P(('seq', 'batch'))
- grad_gain_attn: float32 [768], P(('seq', 'batch'))
- grad_bias_attn: float32 [768], P(('seq', 'batch'))
- grad_gain_ffn: float32 [768], P(('seq', 'batch'))
- grad_bias_ffn: float32 [768], P(('seq', 'batch'))
Inputs may be any that keep to these rules, and one draw needn't show every extreme that they name: `doc_lengths`: every entry is a multiple of 128 and the 4 entries of a sequence add up to 2048. For each sequence index s, in one micro-batch drawn from the seed sequence s is a single document: first entry 2048, the others 0; elsewhere all entries are positive. `random_blocks`: entry [m, s, d * 4 + j, r] names a block of sequence (m, s). With t = (m * 3 + r) * 4 + j, the device along seq that holds the named block (entry // 4) depends only on s, d and t modulo the number of devices along seq, and different residues give different devices. The 3 entries of one block differ.
All inputs are finite; a program needn't handle non-finite values.
Results may differ from a plain program's by a relative error of at most 0.014.
Values may be sent and summed in bfloat16 or wider, within the bound.
A program may use at most 320 MiB of HBM per device.

v0:
```python
import functools

import jax
import jax.numpy as jnp
from jax import lax
from jax.experimental import pallas as pl
from jax.experimental.pallas import tpu as pltpu
from jax.sharding import PartitionSpec as P

F32 = jnp.float32
BF = jnp.bfloat16


HALF, WK, NW, NK, NS = 128, 1152, 1280, 1664, 2304
TOP, REST = 160, 432
MESH = pl.DeviceIdType.MESH
UP, DOWN, XX, YY, CC = range(5)
WAYS = (UP, DOWN, XX, YY, CC)


def dot(a, b):
    return lax.dot_general(a, b, (((1,), (0,)), ((), ())), preferred_element_type=F32)


def dot_nt(a, b):
    return lax.dot_general(a, b, (((1,), (1,)), ((), ())), preferred_element_type=F32)


def dot_tn(a, b):
    return lax.dot_general(a, b, (((0,), (0,)), ((), ())), preferred_element_type=F32)


def place():
    s, b = lax.axis_index("seq"), lax.axis_index("batch")
    return s // 2, s % 2, b // 2, b % 2


def device(z, x, y, c):
    return (2 * z + x, 2 * y + c)


def greet(z, x, y, c):
    barrier = pltpu.get_barrier_semaphore()

    def tell(to):
        pl.semaphore_signal(barrier, inc=1, device_id=to, device_id_type=MESH)

    tell(device(z, 1 - x, y, c))
    tell(device(z, x, 1 - y, c))
    tell(device(z, x, y, 1 - c))
    pl.when(z > 0)(lambda: tell(device(z - 1, x, y, c)))
    pl.when(z < 3)(lambda: tell(device(z + 1, x, y, c)))
    pl.semaphore_wait(barrier, 3 + (z > 0).astype(jnp.int32) + (z < 3).astype(jnp.int32))


def lanes(c):
    return pl.ds(pl.multiple_of(c * 384, 128), 384)


def rows_at(i, n):
    return pl.ds(pl.multiple_of(i * n, n), n)


def remote(src, dst, send, recv, to):
    return pltpu.make_async_remote_copy(
        src_ref=src, dst_ref=dst, send_sem=send, recv_sem=recv, device_id=to, device_id_type=MESH
    )


def key_rows(h):
    return ((HALF * h, WK), (NW + HALF * h, HALF), (NW + 2 * HALF + 384 * h, 384))


def split_heads(v):
    lane = lax.broadcasted_iota(jnp.int32, v.shape, 1)
    z = jnp.zeros_like(v)
    return jnp.concatenate([jnp.where(lane < 64, v, z), jnp.where(lane >= 64, v, z)], axis=0)


def merge_heads(v):
    n = v.shape[0] // 2
    lane = lax.broadcasted_iota(jnp.int32, (n, v.shape[1]), 1)
    return jnp.where(lane < 64, v[:n], v[n:])


def block_columns():
    r = lax.broadcasted_iota(jnp.int32, (2 * HALF, 128), 0)
    lane = lax.broadcasted_iota(jnp.int32, (2 * HALF, 128), 1)
    first = (r % HALF) < 64
    return jnp.where(((lane == 0) & first) | ((lane == 1) & jnp.logical_not(first)), 1.0, 0.0)


def with_column(base, col):
    lane = lax.broadcasted_iota(jnp.int32, base.shape, 1)
    hi = col.astype(BF).astype(F32)
    rest = col - hi
    mid = rest.astype(BF).astype(F32)
    return jnp.where(lane == 2, hi, jnp.where(lane == 3, mid, jnp.where(lane == 4, rest - mid, base))).astype(BF)


def doc_of(lengths, m, block):
    at = block * 64
    doc, first, end = jnp.int32(0), jnp.int32(0), jnp.int32(0)
    for i in range(3):
        end = end + lengths[m, i]
        doc = doc + (end <= at).astype(jnp.int32)
        first = jnp.where(end <= at, end, first)
    return doc, first


def write_extra(lengths, randoms, s, extra):
    lane = lax.broadcasted_iota(jnp.int32, (64, 128), 1)
    ones = jnp.where((lane >= 2) & (lane < 5), 1.0, 0.0)

    def one(i, _):
        m, h, t = i // 52, (i // 26) % 2, i % 26
        r = jnp.maximum(t - 20, 0)
        named = randoms[m, 4 * s + 2 * h + r // 3, r % 3]
        block = jnp.where(t < 18, 4 * s + 2 * h - 8 + t, named)
        inside = (block >= 0) & (block < 32)
        doc, first = doc_of(lengths, m, jnp.clip(block, 0, 31))
        good = inside & (block * 64 - first >= 128)
        terms = []
        for k in range(2):
            query = 4 * s + 2 * h + k
            q_doc, _ = doc_of(lengths, m, query)
            near = jnp.abs(block - query) <= 8
            window = (t < 18) & near
            named_here = (t >= 20) & (r // 3 == k) & jnp.logical_not(near)
            seen = ((t >= 18) & (t < 20)) | (good & (doc == q_doc) & (window | named_here))
            terms.append(jnp.where(seen, 0.0, -1e30))
        value = jnp.where(lane == 0, terms[0], jnp.where(lane == 1, terms[1], ones))
        extra[m, h, rows_at(t, 64), :] = value.astype(BF)
        return 0

    lax.fori_loop(0, 104, one, 0)


def rest_block(lengths, randoms, s, m, t):
    r = jnp.maximum(t - 4, 0)
    named = randoms[m, 4 * s + r // 3, r % 3]
    _, first = doc_of(lengths, m, 4 * s + 2 * jnp.minimum(t // 2, 1))
    return jnp.where(t < 4, first // 64 + t % 2, named)


def forward_kernel(lengths, randoms, x_ref, wq, wk, wv, wo, wu, wd, vectors, b_up,
                   att, lse, q_out, xs_out, k_out, v_out, wall, top_out, bias, extra, targets,
                   own, mate, merged, merged_b, xall0, xall1, xs, ks, vs, wa,
                   mate_sem, lsem, osem, asend, arecv, acrecv, bsend, brecv, bcrecv, xsend, xrecv):
    z, x, y, c = place()
    s = 2 * z + x
    to = {UP: device(z + 1, x, y, c), DOWN: device(z - 1, x, y, c), XX: device(z, 1 - x, y, c),
          YY: device(z, x, 1 - y, c), CC: device(z, x, y, 1 - c)}
    mine, theirs = lanes(c), lanes(1 - c)
    xall = (xall0, xall1)

    def guarded(way, act):
        if way == UP:
            pl.when(z < 3)(act)
        elif way == DOWN:
            pl.when(z > 0)(act)
        else:
            act()

    def x_copy(m, zz, xx, way, own_rows=False):
        i = 2 * zz + xx
        ref = xall[m].at[pl.ds(4 * i, 4)]
        return remote(x_ref.at[m] if own_rows else ref, ref, xsend.at[m, i, way], xrecv.at[m, i], to[way])

    def a_copy(zz, xx, yy, way, src=None):
        i = (2 * zz + xx) * 2 + yy
        ref = wa.at[i, :, mine]
        return remote(ref if src is None else src, ref, asend.at[i, way],
                      acrecv.at[i] if way == CC else arecv.at[i], to[way])

    def b_copy(zz, xx, yy, way, src=None):
        i = (2 * zz + xx) * 2 + yy
        ref = wall.at[i, :, mine]
        return remote(ref if src is None else src, ref, bsend.at[i, way],
                      bcrecv.at[i] if way == CC else brecv.at[i], to[way])

    greet(z, x, y, c)
    for way in (UP, DOWN, XX):
        guarded(way, lambda way=way: x_copy(0, z, x, way, True).start())
    for m in range(2):
        pltpu.make_async_copy(x_ref.at[m], xall[m].at[pl.ds(4 * s, 4)], lsem.at[m]).start()
    owner = 4 * s + 2 * y + c
    small = vectors[...].astype(F32)
    n = small.shape[1]
    own[0:8, :] = pltpu.roll(jnp.concatenate([small, jnp.zeros((8, 768 - n), F32)], axis=1), owner * n, axis=1)
    ups = b_up[...].astype(F32)
    n = ups.shape[1]
    ups = jnp.concatenate([ups, jnp.zeros((1, 768 - n), F32)], axis=1)
    ups = pltpu.roll(jnp.broadcast_to(ups, (8, 768)), (owner % 8) * n, axis=1)
    row = lax.broadcasted_iota(jnp.int32, (8, 768), 0)
    own[8:16, :] = jnp.where(row == owner // 8, ups, 0.0)
    for i, ref in enumerate((wq, wk, wv, wo)):
        own[16 + 24 * i:40 + 24 * i, :] = ref[...].astype(F32)
    for j in range(4):
        own[112 + 24 * j:136 + 24 * j, :] = wu[:, 768 * j:768 * j + 768].astype(F32)
    own[208:304, :] = wd[...].astype(F32)
    swap = remote(own.at[:, theirs], mate, mate_sem.at[0], mate_sem.at[1], to[CC])
    swap.start()
    swap.wait()

    def paired(start, n):
        here, there = own[start:start + n, mine], mate[start:start + n, :]
        return jnp.where(c == 0, jnp.concatenate([here, there], 0), jnp.concatenate([there, here], 0)).astype(BF)

    merged[0:16, :] = (own[0:16, mine] + mate[0:16, :]).astype(BF)
    for i in range(3):
        merged[16 + 48 * i:64 + 48 * i, :] = paired(16 + 24 * i, 24)
    keep_a = pltpu.make_async_copy(merged, wa.at[s * 2 + y, :, mine], lsem.at[2])
    keep_a.start()
    for way in WAYS:
        guarded(way, lambda way=way: a_copy(z, x, y, way, merged).start())
    for i in range(5):
        merged_b[48 * i:48 * i + 48, :] = paired(88 + 24 * i, 24)
    merged_b[240:432, :] = paired(208, 96)
    b_copy(z, x, y, YY, merged_b).start()
    b_copy(z, x, y, CC, merged_b).start()
    keep_b = pltpu.make_async_copy(merged_b, wall.at[s * 2 + y, :, mine], lsem.at[3])
    keep_b.start()
    write_extra(lengths, randoms, s, extra)

    lane = lax.broadcasted_iota(jnp.int32, (1, 1024), 1)
    for m in range(2):
        targets[m] = lax.fori_loop(
            0, 16, lambda t, v, m=m: jnp.where(
                lane // 64 == t, rest_block(lengths, randoms, s, m, t) * 64 + lane % 64, v), jnp.zeros_like(lane))

    def x_line(m, k, a=True):
        def below():
            x_copy(m, z - k, x, UP).wait_recv()
            pl.when(z < 3)(lambda: x_copy(m, z - k, x, UP).start())
            x_copy(m, z - k, x, XX).start()

        def above():
            x_copy(m, z + k, x, DOWN).wait_recv()
            pl.when(z > 0)(lambda: x_copy(m, z + k, x, DOWN).start())
            x_copy(m, z + k, x, XX).start()

        pl.when((z >= k) & (k <= 3))(below)
        pl.when(z + k <= 3)(above)

    def w_line(copy, k):
        def below():
            copy(z - k, x, y, UP).wait_recv()
            pl.when(z < 3)(lambda: copy(z - k, x, y, UP).start())
            for way in (XX, YY, CC):
                copy(z - k, x, y, way).start()

        def above():
            copy(z + k, x, y, DOWN).wait_recv()
            pl.when(z > 0)(lambda: copy(z + k, x, y, DOWN).start())
            for way in (XX, YY, CC):
                copy(z + k, x, y, way).start()

        pl.when((z >= k) & (k <= 3))(below)
        pl.when(z + k <= 3)(above)

    def at_distance(act, k):
        pl.when((k >= 0) & (k <= z))(lambda: act(z - k))
        pl.when((k > 0) & (z + k <= 3))(lambda: act(z + k))

    def w_from_x(copy, k):
        def act(zz):
            copy(zz, 1 - x, y, XX).wait_recv()
            copy(zz, 1 - x, y, YY).start()
            copy(zz, 1 - x, y, CC).start()

        at_distance(act, k)

    def w_from_y(copy, xx, k):
        def act(zz):
            copy(zz, xx, 1 - y, YY).wait_recv()
            copy(zz, xx, 1 - y, CC).start()

        at_distance(act, k)

    zfirst = c == 0

    def b_own_column(k):
        def passed(zz, way, more):
            b_copy(zz, x, y, way).wait_recv()
            pl.when(more)(lambda: b_copy(zz, x, y, way).start())
            b_copy(zz, x, y, YY).start()
            b_copy(zz, x, y, CC).start()

        pl.when((z >= k) & (k <= 3))(lambda: passed(z - k, UP, z < 3))
        pl.when(z + k <= 3)(lambda: passed(z + k, DOWN, z > 0))

    def b_to_x(k):
        def across(zz):
            b_copy(zz, x, y, XX).start()

        pl.when(zfirst)(lambda: at_distance(across, k))

    def b_other_column(k):
        def shared(zz):
            b_copy(zz, 1 - x, y, YY).start()
            b_copy(zz, 1 - x, y, CC).start()

        def crossed(zz):
            b_copy(zz, 1 - x, y, XX).wait_recv()
            shared(zz)

        def passed(zz, way, more):
            b_copy(zz, 1 - x, y, way).wait_recv()
            pl.when(more)(lambda: b_copy(zz, 1 - x, y, way).start())
            shared(zz)

        def first():
            crossed(z)
            pl.when(jnp.logical_not(zfirst) & (z < 3))(lambda: b_copy(z, 1 - x, y, UP).start())
            pl.when(jnp.logical_not(zfirst) & (z > 0))(lambda: b_copy(z, 1 - x, y, DOWN).start())

        def later():
            pl.when(zfirst)(lambda: at_distance(crossed, k))
            pl.when(jnp.logical_not(zfirst) & (z >= k))(lambda: passed(z - k, UP, z < 3))
            pl.when(jnp.logical_not(zfirst) & (z + k <= 3))(lambda: passed(z + k, DOWN, z > 0))

        pl.when(k == 0)(first)
        pl.when((k > 0) & (k <= 3))(later)

    def start_x1(way):
        guarded(way, lambda: x_copy(1, z, x, way, True).start())

    def start_relay(k, _):
        x_line(0, k)
        w_line(a_copy, k)
        w_from_x(a_copy, k - 1)

        @pl.when(k == 2)
        def _():
            start_x1(UP)
            start_x1(DOWN)
            for way in (UP, DOWN):
                guarded(way, lambda way=way: b_copy(z, x, y, way, merged_b).start())

        return 0

    lax.fori_loop(1, 4, start_relay, 0)
    start_x1(XX)
    w_from_x(a_copy, 3)
    x_line(1, 1)
    b_copy(z, x, y, XX, merged_b).start()
    for xx in (x, 1 - x):
        lax.fori_loop(0, 4, lambda k, _, xx=xx: (w_from_y(a_copy, xx, k), 0)[1], 0)
    keep_a.wait()

    def arrived(i, _):
        ref = wa.at[i, :, theirs]
        remote(ref, ref, asend.at[i, CC], acrecv.at[i], to[CC]).wait_recv()
        return 0

    lax.fori_loop(0, 16, arrived, 0)
    bias[...] = jnp.sum(wa[:, 0:16, :].astype(F32), axis=0)
    top_copy = pltpu.make_async_copy(wa, top_out, lsem.at[4])
    top_copy.start()
    lane = lax.broadcasted_iota(jnp.int32, (HALF, 128), 1)
    ind = block_columns().astype(BF)
    lse[...] = jnp.zeros_like(lse)

    def out_copy(m, t):
        src, dst = ((xs, xs_out), (ks, k_out), (vs, v_out))[t]
        return pltpu.make_async_copy(src.at[m], dst.at[m], osem.at[m, t])

    def gather(m):
        def x_here(zz):
            x_copy(m, zz, 1 - x, XX).wait_recv()

        for k in range(4):
            at_distance(x_here, k)
        pltpu.make_async_copy(x_ref.at[m], xall[m].at[pl.ds(4 * s, 4)], lsem.at[m]).wait()
        for t in range(5):
            chunk = xall[m][pl.ds(4 * jnp.clip(s - 2 + t, 0, 7), 4)]
            xs[m, 256 * t:256 * t + 256, :] = chunk.reshape(256, chunk.shape[-1])

        def named(t, _):
            xs[m, pl.ds(pl.multiple_of(NW + 64 * t, 64), 64), :] = xall[m][rest_block(lengths, randoms, s, m, t)]
            return 0

        lax.fori_loop(0, 16, named, 0)
        out_copy(m, 0).start()
        q = (dot(xs[m, 512:768, :], wa[:, 16:64, :].reshape(768, 768)) + bias[0:1, :]).astype(BF)
        q_out[m] = q * jnp.asarray(0.125, BF)

    def project(m, i):
        r = rows_at(i, 768)
        rows = xs[m, r, :]
        ks[m, r, :] = dot(rows, wa[:, 64:112, :].reshape(768, 768)).astype(BF)
        vs[m, r, :] = (dot(rows, wa[:, 112:160, :].reshape(768, 768)) + bias[1:2, :]).astype(BF)

    def pair(m, p):
        col = pl.ds(pl.multiple_of(p * 128, 128), 128)
        for h in range(2):
            r = pl.ds(h * HALF, HALF)
            more = extra[m, h]
            keys = jnp.concatenate([ks[m, a:a + n, col] for a, n in key_rows(h)], axis=0)
            vals = jnp.concatenate([vs[m, a:a + n, col] for a, n in key_rows(h)], axis=0)
            scores = dot_nt(jnp.concatenate([split_heads(q_out[m, r, col]), ind], axis=1),
                            jnp.concatenate([keys, more], axis=1))
            top = jnp.max(scores, axis=1, keepdims=True)
            e = jnp.exp(scores - top).astype(BF)
            o = dot(e, jnp.concatenate([vals, more], axis=1))
            total = o[:, 130:131]
            att[m, r, col] = merge_heads(o[:, :128] / total).astype(BF)
            norm = top + jnp.log(total)
            lse[m, r, :] = jnp.where(lane == 2 * p, norm[:HALF], jnp.where(lane == 2 * p + 1, norm[HALF:], lse[m, r, :]))

    def picked(g, plan):
        k = jnp.full((), 9, jnp.int32)
        for at, value in plan:
            k = jnp.where(g == at, value, k)
        return k

    def pump(g):
        x_line(1, picked(g, PUMP_X))
        b_own_column(picked(g, PUMP_OWN))
        b_other_column(picked(g, PUMP_OTHER))
        b_to_x(picked(g, PUMP_CROSS))
        w_from_y(b_copy, x, picked(g, PUMP_Y0))
        w_from_y(b_copy, 1 - x, picked(g, PUMP_Y1))

    def step(g, _):
        m, i = g // 9, g % 9
        pl.when(g == 0)(lambda: gather(0))
        pl.when(g == 9)(lambda: gather(1))
        pl.when(i < 3)(lambda: project(m, i))

        @pl.when(i == 3)
        def _():
            out_copy(m, 1).start()
            out_copy(m, 2).start()

        pl.when(i >= 3)(lambda: pair(m, i - 3))
        pump(g)
        return 0

    lax.fori_loop(0, 18, step, 0)

    lax.fori_loop(18, 26, lambda g, _: (pump(g), 0)[1], 0)

    def b_arrived(i, _):
        ref = wall.at[i, :, theirs]
        remote(ref, ref, bsend.at[i, CC], bcrecv.at[i], to[CC]).wait_recv()
        return 0

    lax.fori_loop(0, 16, b_arrived, 0)
    keep_b.wait()
    top_copy.wait()
    for m in range(2):
        for t in range(3):
            out_copy(m, t).wait()

    def sent(k, _):
        for m in range(2):
            x_copy(m, k, x, XX).wait_send()
        for copy in (a_copy, b_copy):
            for way in (YY, CC):
                copy(k, x, y, way).wait_send()
                copy(k, 1 - x, y, way).wait_send()
            copy(k, x, 1 - y, CC).wait_send()
            copy(k, 1 - x, 1 - y, CC).wait_send()
        a_copy(k, x, y, XX).wait_send()
        pl.when(zfirst | (k == z))(lambda: b_copy(k, x, y, XX).wait_send())

        def line(way):
            x_copy(0, k, x, way).wait_send()
            x_copy(1, k, x, way).wait_send()
            a_copy(k, x, y, way).wait_send()
            b_copy(k, x, y, way).wait_send()
            pl.when(jnp.logical_not(zfirst))(lambda: b_copy(k, 1 - x, y, way).wait_send())

        pl.when((k <= z) & (z < 3))(lambda: line(UP))
        pl.when((k >= z) & (z > 0))(lambda: line(DOWN))
        return 0

    lax.fori_loop(0, 4, sent, 0)


PUMP_X = ((1, 2), (6, 3))
PUMP_OWN = ((0, 1), (4, 2), (8, 3))
PUMP_OTHER = ((3, 0), (8, 1), (12, 2), (15, 3))
PUMP_CROSS = ((6, 1), (8, 2), (9, 3))
PUMP_Y0 = ((1, 0), (3, 1), (7, 2), (10, 3))
PUMP_Y1 = ((7, 0), (12, 1), (15, 2), (18, 3))


def forward_all(lengths, randoms, x, weights, vectors, b_up):
    dma = pltpu.SemaphoreType.DMA
    sd = jax.ShapeDtypeStruct
    vm, anywhere, sm = (pl.BlockSpec(memory_space=m) for m in (pltpu.VMEM, pl.ANY, pltpu.SMEM))
    mb, rows, width = x.shape
    v = pltpu.VMEM
    return pl.pallas_call(
        forward_kernel,
        out_shape=[
            sd((mb, rows, width), BF), sd((mb, rows, 128), F32), sd((mb, rows, width), BF),
            sd((mb, NS, width), BF), sd((mb, NS, width), BF), sd((mb, NS, width), BF),
            sd((16, REST, width), BF), sd((16, TOP, width), BF), sd((16, width), F32),
            sd((mb, 2, NK, 128), BF), sd((mb, 1, 1024), jnp.int32),
        ],
        in_specs=[sm, sm, anywhere] + [vm] * 8,
        out_specs=[vm, vm, vm, anywhere, anywhere, anywhere, anywhere, anywhere, vm, vm, vm],
        scratch_shapes=[
            v((304, width), F32), v((304, 384), F32), v((TOP, 384), BF), v((REST, 384), BF),
            v((8 * rows // 64, 64, width), BF), v((8 * rows // 64, 64, width), BF),
            v((mb, NS, width), BF), v((mb, NS, width), BF), v((mb, NS, width), BF),
            v((16, TOP, width), BF),
            dma((2,)), dma((5,)), dma((mb, 3)),
            dma((16, 5)), dma((16,)), dma((16,)), dma((16, 5)), dma((16,)), dma((16,)),
            dma((mb, 8, 3)), dma((mb, 8)),
        ],
        compiler_params=pltpu.CompilerParams(
            collective_id=0, has_side_effects=True, vmem_limit_bytes=60 * 2**20
        ),
    )(lengths, randoms, x.reshape(mb, rows // 64, 64, width), *weights, vectors, b_up)


def backward_kernel(datt, stats, tgt, gb_in, extra_in, q_in, done, k_in, v_in, xs_in, top_in, go, gu, gd,
                    oq, ok, ov, oo, ou, od, ob, odx,
                    kb, vb, xsb, wa, extra, dka, dva, q, ga, gb,
                    acc, mate, yr, mate2, yr2, xr, zr, dxp, dxr, dzr, fin, rcv,
                    ksem, lsem, msem, msem2, asem, ysem, xsem, zsem, ysem2, xsem2, zsem2, dxsem, dzsem, fsem, ready):
    z, x, y, c = place()
    s = 2 * z + x
    mine, theirs = lanes(c), lanes(1 - c)
    near_x, near_y, near_c = device(z, 1 - x, y, c), device(z, x, 1 - y, c), device(z, x, y, 1 - c)
    above, below = device(z + 1, x, y, c), device(z - 1, x, y, c)

    def far(i):
        inner = jnp.where(i == 0, 3, jnp.where(i == 1, 0, jnp.where(i == 2, 2, 1)))
        low = jnp.where(z == 0, 3 - i, jnp.where(z == 1, inner, i))
        return jnp.where(z == 2, 3 - inner, low)

    def slot_of(i, zz):
        zt = jnp.where(zz == 0, 3 - i, jnp.where((zz == 1) & (i == 2), 2, 3))
        return zt, (zz == 0) | ((zz == 1) & (i >= 1)) | ((zz == 2) & (i == 2))

    def at_slot(act, i):
        up, sends_up = slot_of(i, z)
        down, sends_down = slot_of(i, 3 - z)
        pl.when(sends_up)(lambda: act(up, True))
        pl.when(sends_down)(lambda: act(3 - down, False))

    def column(p):
        return pl.ds(pl.multiple_of(p * 128, 128), 128)

    def load_keys(m, p):
        return (pltpu.make_async_copy(k_in.at[m, :, column(p)], kb.at[:, column(p)], ksem.at[0, p]),
                pltpu.make_async_copy(v_in.at[m, :, column(p)], vb.at[:, column(p)], ksem.at[1, p]))

    def start_keys(m):
        def one(p, _):
            for cp in load_keys(m, p):
                cp.start()
            return 0

        lax.fori_loop(0, 6, one, 0)

    start_keys(0)
    extra_copy = pltpu.make_async_copy(extra_in, extra, lsem.at[4])
    extra_copy.start()
    q_copy = pltpu.make_async_copy(q_in, q, lsem.at[3])
    q_copy.start()
    top_copy = pltpu.make_async_copy(top_in.at[:, :, pl.ds(16, 144), :], wa, lsem.at[0])
    top_copy.start()
    done_copy = pltpu.make_async_copy(done, odx, lsem.at[1])
    done_copy.start()
    greet(z, x, y, c)

    def parts(yy, cc):
        off = pl.multiple_of(cc * 384, 128)
        yield 0, go.at[:, yy, :, pl.ds(off, 384)], pl.ds(0, 48)
        yield 1, gd.at[:, yy, :, pl.ds(off, 384)], pl.ds(240, 192)
        for j in range(4):
            col = pl.multiple_of(j * 768 + cc * 384, 128)
            yield 2 + j, gu.at[:, yy, :, pl.ds(col, 384)], pl.ds(48 + 48 * j, 48)

    swaps, loads = {}, {}
    for t, yy in enumerate((1 - y, y)):
        for i, src, rows in parts(yy, 1 - c):
            swaps[t, i] = remote(src, mate.at[:, yy, rows, :], msem.at[0, t, i], msem.at[1, t, i], near_c)
            swaps[t, i].start()
        for i, src, rows in parts(yy, c):
            loads[t, i] = pltpu.make_async_copy(src, acc.at[:, yy, rows, :], asem.at[t, i])
            loads[t, i].start()
    gb[...] = gb_in[...]

    class Reduce:
        def __init__(self, rows, held, cols, other, from_y, ys, xs_, zs):
            self.rows, self.held, self.cols, self.other, self.from_y = rows, held, cols, other, from_y
            self.ys, self.xs, self.zs = ys, xs_, zs

        def a(self, s_, yy):
            return self.held.at[s_, yy, :, self.cols]

        def y_copy(self, s_):
            return remote(self.a(s_, 1 - y), self.from_y.at[s_], self.ys.at[0, s_], self.ys.at[1, s_], near_y)

        def x_copy(self, zz):
            return remote(self.a(2 * zz + 1 - x, y), xr.at[zz, pl.ds(0, self.rows), :], self.xs.at[0, zz],
                          self.xs.at[1, zz], near_x)

        def z_copy(self, zz, slot, to):
            return remote(self.a(2 * zz + x, y), zr.at[slot, pl.ds(0, self.rows), :], self.zs.at[0, zz],
                          self.zs.at[1, slot], to)

        def total(self, s_, yy, others):
            value = self.held[s_, yy, :, self.cols].astype(F32) + self.other[s_, yy].astype(F32)
            for ref, index in others:
                value = value + ref[index, 0:self.rows, :].astype(F32)
            return value

        def keep(self, s_, yy, value):
            self.held[s_, yy, :, self.cols] = value.astype(BF)

        def y_step(self, i):
            s_ = 2 * far(i % 4) + jnp.where(i < 4, 1 - x, x)
            self.keep(s_, 1 - y, self.total(s_, 1 - y, []))
            self.y_copy(s_).start()

        def x_step(self, i):
            zz = far(i)
            s_ = 2 * zz + 1 - x
            self.y_copy(s_).wait_recv()
            self.keep(s_, y, self.total(s_, y, [(self.from_y, s_)]))
            self.x_copy(zz).start()

        def along(self, zz, up):
            s_ = 2 * zz + x
            self.y_copy(s_).wait_recv()
            self.x_copy(zz).wait_recv()
            others = [(self.from_y, s_), (xr, zz)]
            more = z > 0 if up else z < 3

            @pl.when(more)
            def _():
                self.z_copy(zz, zz, above).wait_recv()
                self.keep(s_, y, self.total(s_, y, others + [(zr, zz)]))

            @pl.when(jnp.logical_not(more))
            def _():
                self.keep(s_, y, self.total(s_, y, others))

            if up:
                self.z_copy(zz, zz, above).start()
            else:
                self.z_copy(zz, jnp.where(zz == z - 1, 4, zz), below).start()

        def z_step(self, i):
            at_slot(self.along, i)

        def finish(self):
            self.y_copy(s).wait_recv()
            self.x_copy(z).wait_recv()
            r = pl.ds(0, self.rows)
            fin[r, :] = self.total(s, y, [(self.from_y, s), (xr, z)])
            for slot, cond in ((z, z > 0), (4, z < 3)):
                @pl.when(cond)
                def _(slot=slot):
                    self.z_copy(z, slot, above).wait_recv()
                    fin[r, :] += zr[slot, r, :].astype(F32)

        def drain(self):
            def one(i, _):
                self.y_copy(i).wait_send()
                return 0

            lax.fori_loop(0, 8, one, 0)

            def two(i, _):
                self.x_copy(i).wait_send()
                pl.when(i != z)(lambda: self.z_copy(i, i, above).wait_send())
                return 0

            lax.fori_loop(0, 4, two, 0)

    rest = Reduce(REST, acc, pl.ds(0, 384), mate, yr, ysem, xsem, zsem)
    top = Reduce(TOP, ga, mine, mate2, yr2, ysem2, xsem2, zsem2)

    def dx_x(m, zz):
        return remote(dxp.at[m, 2 * zz + 1 - x], dxr.at[m, zz], dxsem.at[0, m, zz], dxsem.at[1, m, zz], near_x)

    def dx_z(m, zz, slot, to):
        return remote(dxp.at[m, 2 * zz + x], dzr.at[m, slot], dzsem.at[0, m, zz], dzsem.at[1, m, slot], to)

    def dx_along(m, zz, up):
        s_ = 2 * zz + x
        dx_x(m, zz).wait_recv()
        more = z > 0 if up else z < 3

        @pl.when(more)
        def _():
            dx_z(m, zz, zz, above).wait_recv()
            dxp[m, s_] = (dxp[m, s_].astype(F32) + dxr[m, zz].astype(F32) + dzr[m, zz].astype(F32)).astype(BF)

        @pl.when(jnp.logical_not(more))
        def _():
            dxp[m, s_] = (dxp[m, s_].astype(F32) + dxr[m, zz].astype(F32)).astype(BF)

        if up:
            dx_z(m, zz, zz, above).start()
        else:
            dx_z(m, zz, jnp.where(zz == z - 1, 4, zz), below).start()

    def dx_step(m, i):
        at_slot(functools.partial(dx_along, m), i)

    def dx_finish(m):
        dx_x(m, z).wait_recv()
        odx[m] += dxr[m, z].astype(F32)
        for slot, cond in ((z, z > 0), (4, z < 3)):
            @pl.when(cond)
            def _(slot=slot):
                dx_z(m, z, slot, above).wait_recv()
                odx[m] += dzr[m, slot].astype(F32)

    def dx_sent(m):
        def one(i, _):
            dx_x(m, i).wait_send()
            pl.when(i != z)(lambda: dx_z(m, i, i, above).wait_send())
            return 0

        lax.fori_loop(0, 4, one, 0)

    ind = block_columns()

    def pair(m, p):
        col = column(p)
        for cp in load_keys(m, p):
            cp.wait()
        dka[...] = jnp.zeros_like(dka)
        dva[...] = jnp.zeros_like(dva)
        for h in range(2):
            rows = pl.ds(h * HALF, HALF)
            qs = split_heads(q[m, rows, col])
            dos = split_heads(datt[m, rows, col])
            lane = lax.broadcasted_iota(jnp.int32, (HALF, 128), 1)

            def both(first, rows=rows, lane=lane):
                return jnp.concatenate(
                    [jnp.sum(jnp.where(lane == first + a, stats[m, rows, :], 0.0), axis=1, keepdims=True) for a in range(2)],
                    axis=0)

            log_norm, delta = both(2 * p), both(16 + 2 * p)
            qe = jnp.concatenate([qs, with_column(ind, -log_norm)], axis=1)
            doe = jnp.concatenate([dos, with_column(jnp.zeros_like(ind), -delta)], axis=1)
            dqt = jnp.zeros((128, 2 * HALF), F32)
            (wa_, wn), (ga, gn), (ra, rn) = key_rows(h)
            off = 0
            for pieces in (((wa_, 576),), ((wa_ + 576, 576),), ((ga, gn), (ra, rn))):
                n = sum(t for _, t in pieces)
                k2 = jnp.concatenate([kb[a:a + t, col] for a, t in pieces], axis=0)
                v2 = jnp.concatenate([vb[a:a + t, col] for a, t in pieces], axis=0)
                more = extra[m, h, off:off + n, :]
                pt = jnp.exp(dot_nt(jnp.concatenate([k2, more], axis=1), qe))
                ds = (pt * dot_nt(jnp.concatenate([v2, more], axis=1), doe)).astype(BF)
                dv_ = dot(pt.astype(BF), dos)
                dk_ = dot(ds, qs)
                dqt = dqt + dot(k2.T, ds)
                if off < WK:
                    a, t = pieces[0]
                    dka[a:a + t, :] += dk_
                    dva[a:a + t, :] += dv_
                else:
                    at = 0
                    for a, t in pieces:
                        kb[a:a + t, col] = dk_[at:at + t].astype(BF)
                        vb[a:a + t, col] = dv_[at:at + t].astype(BF)
                        at += t
                off += n
            q[m, rows, col] = (merge_heads(dqt.T) * 0.125).astype(BF)
        kb[0:NW, col] = dka[...].astype(BF)
        vb[0:NW, col] = dva[...].astype(BF)

    def weight(i):
        return wa[:, :, 48 * i:48 + 48 * i, :].reshape(768, 768)

    def dx_rows(m, i):
        for part in range(2):
            r = rows_at(2 * i + part, 384)
            value = dot_nt(kb[r, :], weight(1)) + dot_nt(vb[r, :], weight(2))
            xsb[r, :] = value.astype(BF)
            if part == 1:
                @pl.when(i == 0)
                def _(value=value):
                    odx[m] += value[128:384] + dot_nt(q[m], weight(0))

    def dx_piece(m, i):
        t = 2 * far(i % 4) + jnp.where(i < 4, 1 - x, x)
        row = lax.broadcasted_iota(jnp.int32, (256, 1024), 0) + 256 * t
        chosen = jnp.where(row == tgt[m], 1.0, 0.0).astype(BF)
        value = dot(chosen, xsb[NW:NS, :])
        w = t - s + 2

        @pl.when(t == s)
        def _():
            odx[m] += value

        @pl.when(t != s)
        def _():
            near = xsb[rows_at(jnp.clip(w, 0, 4), 256), :].astype(F32)
            dxp[m, t] = (value + jnp.where((w >= 0) & (w < 5), near, 0.0)).astype(BF)

        pl.when(i < 4)(lambda: dx_x(m, far(i % 4)).start())

    def weight_grads(m, i):
        cols = pl.ds(pl.multiple_of(384 * i, 128), 384)
        a = xsb[:, cols]
        chips = pl.ds(4 * i, 4)

        def keep(row, value, n):
            value = value.reshape(4, 2, 48, value.shape[1])

            @pl.when(m == 0)
            def _():
                ga[chips, :, row:row + 48, n] = value.astype(BF)

            @pl.when(m == 1)
            def _():
                ga[chips, :, row:row + 48, n] = (ga[chips, :, row:row + 48, n].astype(F32) + value).astype(BF)

        for half in range(2):
            n = slice(384 * half, 384 * half + 384)
            keep(64, dot_tn(a, kb[:, n]), n)
            keep(112, dot_tn(a, vb[:, n]), n)
        keep(16, dot_tn(a[512:768], q[m]), slice(0, 768))

    def small_grads():
        low = gb[...].astype(BF)

        def spread(i, _):
            ga[i // 2, i % 2, 0:16, :] = low
            return 0

        lax.fori_loop(0, 16, spread, 0)

    swap2 = [remote(ga.at[:, yy, :, theirs], mate2.at[:, yy], msem2.at[0, t], msem2.at[1, t], near_c)
             for t, yy in enumerate((1 - y, y))]

    def picked(g, plan):
        k = jnp.full((), 9, jnp.int32)
        for at, value in plan:
            k = jnp.where(g == at, value, k)
        return k

    def pump(g):
        k = picked(g, PLAN_Y)
        pl.when(k < 9)(lambda: rest.y_step(k))
        k2 = picked(g, PLAN_X)
        pl.when(k2 < 9)(lambda: rest.x_step(k2))
        k3 = picked(g, PLAN_D)
        pl.when(k3 < 3)(lambda: dx_step(0, k3))
        k4 = picked(g, PLAN_Z)
        pl.when(k4 < 3)(lambda: rest.z_step(k4))

        def start_top():
            swap2[0].wait_recv()
            swap2[1].wait_recv()
            lax.fori_loop(0, 8, lambda i, _: (top.y_step(i), 0)[1], 0)

        pl.when(g == PLAN_TOP)(start_top)

    for i in range(6):
        loads[0, i].wait()
        swaps[0, i].wait_recv()
    rest.y_step(0)
    done_copy.wait()
    q_copy.wait()
    extra_copy.wait()

    def load_xs(m):
        return pltpu.make_async_copy(xs_in.at[m], xsb, lsem.at[2])

    def micro(m, _):
        load_xs(m).start()

        def pairs(p, _):
            pair(m, p)

            @pl.when((m == 0) & (p == 4))
            def _():
                for i in range(6):
                    loads[1, i].wait()
                    swaps[1, i].wait_recv()
                top_copy.wait()

            pump(12 * m + p)
            return 0

        lax.fori_loop(0, 6, pairs, 0)
        load_xs(m).wait()

        def grads(i, _):
            weight_grads(m, i)
            pump(12 * m + 6 + i)
            return 0

        lax.fori_loop(0, 2, grads, 0)
        gb[0:1, :] += jnp.sum(q[m].astype(F32), axis=0, keepdims=True)

        def value_bias(i, _):
            gb[1:2, :] += jnp.sum(vb[rows_at(i, 256), :].astype(F32), axis=0, keepdims=True)
            return 0

        lax.fori_loop(0, 9, value_bias, 0)
        pump(12 * m + 8)

        @pl.when(m == 1)
        def _():
            small_grads()
            for cp in swap2:
                cp.start()

        def rows(i, _):
            dx_rows(m, i)
            pump(12 * m + 9 + i)
            return 0

        lax.fori_loop(0, 3, rows, 0)
        pl.when(m == 0)(lambda: start_keys(1))
        lax.fori_loop(0, 8, lambda i, _: (dx_piece(m, i), 0)[1], 0)
        return 0

    lax.fori_loop(0, 2, micro, 0)

    def rest_rows(cc):
        yield oo, 0, pl.multiple_of(24 * cc, 8), 24, 0
        for j in range(4):
            yield ou, 24 + 24 * j, pl.multiple_of(48 + 48 * j + 24 * cc, 8), 24, 768 * j
        yield od, 120, pl.multiple_of(240 + 96 * cc, 8), 96, 0

    def top_rows(cc):
        yield ob, 216, 0, 16, 0
        for i, ref in enumerate((oq, ok, ov)):
            yield ref, 232 + 24 * i, pl.multiple_of(16 + 48 * i + 24 * cc, 8), 24, 0

    def to_mate(rows_of, first):
        return [remote(fin.at[pl.ds(start, n), :], rcv.at[at:at + n, :], fsem.at[0, first + i], fsem.at[1, first + i], near_c)
                for i, (_, at, start, n, _) in enumerate(rows_of(1 - c))]

    def hand_over(rows_of):
        for ref, at, start, n, col in rows_of(c):
            ref[:, pl.ds(pl.multiple_of(col + c * 384, 128), 384)] = fin[pl.ds(start, n), :]

    def take_over(rows_of):
        for ref, at, start, n, col in rows_of(c):
            ref[:, pl.ds(pl.multiple_of(col + (1 - c) * 384, 128), 384)] = rcv[at:at + n, :]

    def tell(to):
        pl.semaphore_signal(ready, inc=1, device_id=to, device_id_type=MESH)

    last0 = to_mate(rest_rows, 0)

    def tail(g, _):
        def step(plan, act):
            k = picked(g, plan)
            pl.when(k < 9)(lambda: act(k))

        @pl.when(g == TAIL_B)
        def _():
            rest.finish()
            for to in (near_x, near_y, near_c):
                tell(to)
            pl.when(z > 0)(lambda: tell(below))
            pl.when(z < 3)(lambda: tell(above))
            for cp in last0:
                cp.start()
            hand_over(rest_rows)

        @pl.when(g == TAIL_W)
        def _():
            pl.semaphore_wait(ready, 3 + (z > 0).astype(jnp.int32) + (z < 3).astype(jnp.int32))

        step(TAIL_D0, lambda k: dx_step(0, k))
        pl.when(g == TAIL_D0_END)(lambda: dx_finish(0))
        step(TAIL_X, top.x_step)
        step(TAIL_D, lambda k: dx_step(1, k))
        step(TAIL_Z, top.z_step)
        return 0

    lax.fori_loop(0, TAIL, tail, 0)
    dx_finish(1)
    for cp in last0:
        cp.wait()
    take_over(rest_rows)
    top.finish()
    last1 = to_mate(top_rows, 6)
    for cp in last1:
        cp.start()
    hand_over(top_rows)
    for cp in last1:
        cp.wait()
    take_over(top_rows)
    top.drain()
    rest.drain()
    for t in range(2):
        for i in range(6):
            swaps[t, i].wait_send()
    dx_sent(0)
    dx_sent(1)
    for cp in swap2:
        cp.wait_send()


PLAN_Y = ((0, 1), (1, 2), (2, 3), (3, 4), (4, 5), (5, 6), (6, 7))
PLAN_X = ((5, 0), (6, 1), (8, 2), (11, 3))
PLAN_Z = ((13, 0), (16, 1), (19, 2))
PLAN_D = ((16, 0), (20, 1), (23, 2))
PLAN_TOP = 21
TAIL_B = 0
TAIL_W = 1
TAIL_D0 = ()
TAIL_D0_END = 1
TAIL_X = ((1, 0), (2, 1), (3, 2), (4, 3))
TAIL_D = ((1, 0), (3, 1), (5, 2))
TAIL_Z = ((4, 0), (5, 1), (6, 2))
TAIL = 7


def backward_all(datt, stats, tgt, gb, extra, q, done, k, v, xs, top, go, gu, gd):
    dma = pltpu.SemaphoreType.DMA
    sd = jax.ShapeDtypeStruct
    vm, anywhere = (pl.BlockSpec(memory_space=m) for m in (pltpu.VMEM, pl.ANY))
    mb, rows, width = q.shape
    s = pltpu.VMEM
    views = [top.reshape(8, 2, TOP, width), go.reshape(8, 2, 48, width), gu.reshape(8, 2, 48, 4 * width),
             gd.reshape(8, 2, 192, width)]
    return pl.pallas_call(
        backward_kernel,
        out_shape=[sd((24, width), F32)] * 4 + [sd((24, 4 * width), F32), sd((96, width), F32), sd((16, width), F32),
                                                sd(q.shape, F32)],
        in_specs=[vm] * 4 + [anywhere] * 10,
        out_specs=[vm] * 8,
        scratch_shapes=[
            s((NS, width), BF), s((NS, width), BF), s((NS, width), BF), s((8, 2, TOP - 16, width), BF),
            s((mb, 2, NK, 128), BF), s((NW, 128), F32), s((NW, 128), F32), s((mb, rows, width), BF),
            s((8, 2, TOP, width), BF), s((16, width), F32),
            s((8, 2, REST, 384), BF), s((8, 2, REST, 384), BF), s((8, REST, 384), BF), s((8, 2, TOP, 384), BF), s((8, TOP, 384), BF),
            s((4, REST, 384), BF),
            s((5, REST, 384), BF),
            s((mb, 8, rows, width), BF), s((mb, 4, rows, width), BF), s((mb, 5, rows, width), BF),
            s((REST, 384), F32), s((304, 384), F32),
            dma((2, 6)), dma((5,)), dma((2, 2, 6)), dma((2, 2)), dma((2, 6)),
            dma((2, 8)), dma((2, 4)), dma((2, 5)), dma((2, 8)), dma((2, 4)), dma((2, 5)),
            dma((2, mb, 4)), dma((2, mb, 5)), dma((2, 10)), pltpu.SemaphoreType.REGULAR,
        ],
        compiler_params=pltpu.CompilerParams(
            collective_id=1, has_side_effects=True, vmem_limit_bytes=62 * 2**20
        ),
    )(datt, stats, tgt, gb, extra, q, done, k, v, xs, *views)


CHUNKS = 9


def project_kernel(idx, xall, wall, bias, xs_ref, k_ref, v_ref, q_ref, xs, w, sems, wsem):
    m, i = pl.program_id(0), pl.program_id(1)

    @pl.when((m == 0) & (i == 0))
    def _():
        copy = pltpu.make_async_copy(wall.at[:, pl.ds(16, 144), :], w, wsem)
        copy.start()
        for mm in range(2):
            for cc in range(CHUNKS):
                pieces = [(0, 256)] if cc < 5 else [(0, 128), (128, 128)] if cc == 5 else [(64 * t, 64) for t in range(4)]
                base = cc if cc < 5 else 5 if cc == 5 else 7 + 4 * (cc - 6)
                for t, (off, n) in enumerate(pieces):
                    start = pl.multiple_of(idx[mm, base + t], 64)
                    pltpu.make_async_copy(xall.at[mm, pl.ds(start, n), :], xs.at[mm, cc, pl.ds(off, n), :],
                                          sems.at[mm, cc]).start()
        copy.wait()

    pltpu.make_async_copy(xall.at[0, pl.ds(0, 256), :], xs.at[m, i], sems.at[m, i]).wait()
    rows = xs[m, i]
    xs_ref[0] = rows
    k_ref[0] = dot(rows, w[:, 48:96, :].reshape(768, 768)).astype(BF)
    v_ref[0] = (dot(rows, w[:, 96:144, :].reshape(768, 768)) + bias[1:2, :]).astype(BF)

    @pl.when(i == 2)
    def _():
        q = (dot(rows, w[:, 0:48, :].reshape(768, 768)) + bias[0:1, :]).astype(BF)
        q_ref[0] = q * jnp.asarray(0.125, BF)


def project(idx, xall, wall, bias):
    mb = xall.shape[0]
    sd = jax.ShapeDtypeStruct
    chunk = pl.BlockSpec((1, 256, 768), lambda m, i, t: (m, i, 0))
    return pl.pallas_call(
        project_kernel,
        grid_spec=pltpu.PrefetchScalarGridSpec(
            num_scalar_prefetch=1,
            grid=(mb, CHUNKS),
            in_specs=[pl.BlockSpec(memory_space=pl.ANY)] * 2 + [pl.BlockSpec((16, 768), lambda m, i, t: (0, 0))],
            out_specs=[chunk, chunk, chunk, pl.BlockSpec((1, 256, 768), lambda m, i, t: (m, 0, 0))],
            scratch_shapes=[
                pltpu.VMEM((mb, CHUNKS, 256, 768), BF), pltpu.VMEM((16, 144, 768), BF),
                pltpu.SemaphoreType.DMA((mb, CHUNKS)), pltpu.SemaphoreType.DMA,
            ],
        ),
        out_shape=[sd((mb, NS, 768), BF)] * 3 + [sd((mb, 256, 768), BF)],
        compiler_params=pltpu.CompilerParams(vmem_limit_bytes=48 * 2**20),
    )(idx, xall, wall, bias)


EPS = 1e-6
G0, G1 = 0.7978845608, 0.044715


def norm(v):
    mean = jnp.mean(v, axis=-1, keepdims=True)
    centred = v - mean
    inverse = lax.rsqrt(jnp.mean(centred * centred, axis=-1, keepdims=True) + EPS)
    return centred * inverse, inverse


def norm_back(g, normed, inverse, gain):
    c = g * gain
    return inverse * (c - jnp.mean(c, axis=-1, keepdims=True)
                      - normed * jnp.mean(c * normed, axis=-1, keepdims=True))


def middle_kernel(att, x, cot, wall, bias, lse, out_ref, stats_ref, datt_ref, done_ref, go_out, gu_out, gd_out, gb_ref,
                  go_ref, gu_ref, gd_ref, gsem, w, wsem, pre, hid, mid, low, n1, r1, ffn):
    rows = x.shape[0]
    copies = [
        pltpu.make_async_copy(wall.at[:, pl.ds(0, 48), :], w.at[:, pl.ds(0, 48), :], wsem.at[0]),
        pltpu.make_async_copy(wall.at[:, pl.ds(48, 192), :], w.at[:, pl.ds(48, 192), :], wsem.at[1]),
        pltpu.make_async_copy(wall.at[:, pl.ds(240, 192), :], w.at[:, pl.ds(240, 192), :], wsem.at[2]),
    ]
    for cp in copies:
        cp.start()
    half = rows // 2
    copies[0].wait()
    w_out = w[:, 0:48, :].reshape(768, 768)
    for h in range(2):
        r = pl.ds(h * half, half)
        t = x[r, :].astype(F32) + dot(att[r, :], w_out) + bias[2:3, :]
        normed, inverse = norm(t)
        n1[r, :] = normed
        r1[r, :] = jnp.broadcast_to(inverse, (half, 128))
        value = normed * bias[4:5, :] + bias[5:6, :]
        mid[r, :] = value
        low[r, :] = value.astype(BF)
    ffn[...] = jnp.broadcast_to(bias[3:4, :], ffn.shape)
    copies[1].wait()
    copies[2].wait()

    def up_block(j):
        return w[:, pl.ds(pl.multiple_of(48 + 48 * j, 16), 48), :].reshape(768, 768)

    def down_block(j):
        return w[pl.ds(4 * j, 4), 240:432, :].reshape(768, 768)

    def forward(j, _):
        wu, wd = up_block(j), down_block(j)
        for h in range(2):
            r = pl.ds(h * half, half)
            u = dot(low[r, :], wu) + bias[pl.ds(8 + j, 1), :]
            pre[j, r, :] = u
            g = (0.5 * u * (1.0 + jnp.tanh(G0 * (u + G1 * u * u * u)))).astype(BF)
            hid[j, r, :] = g
            ffn[r, :] += dot(g, wd)
        return 0

    lax.fori_loop(0, 4, forward, 0)
    gb_ref[...] = jnp.zeros_like(gb_ref)
    for h in range(2):
        r = pl.ds(h * half, half)
        normed, inverse = norm(mid[r, :] + ffn[r, :])
        out_ref[r, :] = (normed * bias[6:7, :] + bias[7:8, :]).astype(BF)
        g = cot[r, :].astype(F32)
        gb_ref[6:7, :] += jnp.sum(g * normed, axis=0, keepdims=True)
        gb_ref[7:8, :] += jnp.sum(g, axis=0, keepdims=True)
        d_two = norm_back(g, normed, inverse, bias[6:7, :])
        mid[r, :] = d_two
        d_ffn = d_two.astype(BF)
        datt_ref[r, :] = d_ffn
        gb_ref[3:4, :] += jnp.sum(d_ffn.astype(F32), axis=0, keepdims=True)

    def sent(ref, out, j, t):
        at = pl.ds(pl.multiple_of(j * 768, 768), 768)
        return pltpu.make_async_copy(ref.at[j], out.at[at, :] if t == 0 else out.at[:, at], gsem.at[t, j])

    def backward(j, _):
        wu, wd = up_block(j), down_block(j)
        d_ffn = datt_ref[...]
        gd_ref[j] = dot_tn(hid[j], d_ffn).astype(BF)
        sent(gd_ref, gd_out, j, 0).start()
        for h in range(2):
            r = pl.ds(h * half, half)
            u = pre[j, r, :]
            th = jnp.tanh(G0 * (u + G1 * u * u * u))
            slope = 0.5 * (1.0 + th) + 0.5 * u * (1.0 - th * th) * (G0 * (1.0 + 3.0 * G1 * u * u))
            d_pre = (dot_nt(datt_ref[r, :], wd) * slope).astype(BF)
            hid[j, r, :] = d_pre
            gb_ref[pl.ds(8 + j, 1), :] += jnp.sum(d_pre.astype(F32), axis=0, keepdims=True)
            mid[r, :] += dot_nt(d_pre, wu)
        gu_ref[j] = dot_tn(low[...], hid[j]).astype(BF)
        sent(gu_ref, gu_out, j, 1).start()
        return 0

    lax.fori_loop(0, 4, backward, 0)
    for h in range(2):
        r = pl.ds(h * half, half)
        d_mid, normed = mid[r, :], n1[r, :]
        gb_ref[4:5, :] += jnp.sum(d_mid * normed, axis=0, keepdims=True)
        gb_ref[5:6, :] += jnp.sum(d_mid, axis=0, keepdims=True)
        d_one = norm_back(d_mid, normed, r1[r, 0:1], bias[4:5, :])
        done_ref[r, :] = d_one
        d_branch = d_one.astype(BF)
        low[r, :] = d_branch
        gb_ref[2:3, :] += jnp.sum(d_branch.astype(F32), axis=0, keepdims=True)
        d_att = dot_nt(d_branch, w_out).astype(BF)
        datt_ref[r, :] = d_att
        product = d_att.astype(F32) * att[r, :].astype(F32)
        lane = lax.broadcasted_iota(jnp.int32, (half, 128), 1)
        stats = lse[r, :]
        for p in range(6):
            two = product[:, 128 * p:128 * p + 128]
            stats = jnp.where(lane == 16 + 2 * p, jnp.sum(jnp.where(lane < 64, two, 0.0), axis=1, keepdims=True), stats)
            stats = jnp.where(lane == 17 + 2 * p, jnp.sum(jnp.where(lane >= 64, two, 0.0), axis=1, keepdims=True), stats)
        stats_ref[r, :] = stats
    go_ref[...] = dot_tn(att[...], low[...]).astype(BF)
    go_copy = pltpu.make_async_copy(go_ref, go_out, wsem.at[0])
    go_copy.start()
    for j in range(4):
        sent(gd_ref, gd_out, j, 0).wait()
        sent(gu_ref, gu_out, j, 1).wait()
    go_copy.wait()


def middle(att, x, cot, wall, bias, lse):
    rows = x.shape[0]
    sd = jax.ShapeDtypeStruct
    vm = pl.BlockSpec(memory_space=pltpu.VMEM)
    return pl.pallas_call(
        middle_kernel,
        in_specs=[vm, vm, vm, pl.BlockSpec(memory_space=pl.ANY), vm, vm],
        out_specs=[vm] * 4 + [pl.BlockSpec(memory_space=pl.ANY)] * 3 + [vm],
        out_shape=[sd((rows, 768), BF), sd((rows, 128), F32), sd((rows, 768), BF), sd((rows, 768), F32), sd((768, 768), BF),
                   sd((768, 3072), BF), sd((3072, 768), BF), sd((16, 768), F32)],
        scratch_shapes=[
            pltpu.VMEM((768, 768), BF), pltpu.VMEM((4, 768, 768), BF), pltpu.VMEM((4, 768, 768), BF),
            pltpu.SemaphoreType.DMA((2, 4)),
            pltpu.VMEM((16, 432, 768), BF), pltpu.SemaphoreType.DMA((3,)),
            pltpu.VMEM((4, rows, 768), F32), pltpu.VMEM((4, rows, 768), BF),
            pltpu.VMEM((rows, 768), F32), pltpu.VMEM((rows, 768), BF), pltpu.VMEM((rows, 768), F32),
            pltpu.VMEM((rows, 128), F32), pltpu.VMEM((rows, 768), F32),
        ],
        compiler_params=pltpu.CompilerParams(vmem_limit_bytes=60 * 2**20),
    )(att, x, cot, wall, bias, lse)


def back_kernel(scattered, idx, xs_ref, dk_ref, dv_ref, dq_ref, done_ref, wall, gb_in, dx_ref, own_ref, gq_ref, gk_ref, gv_ref, gb_ref,
                w, wsem, acc, aq, ak, av):
    m, i = pl.program_id(0), pl.program_id(1)

    @pl.when((m == 0) & (i == 0))
    def _():
        copy = pltpu.make_async_copy(wall.at[:, pl.ds(16, 144), :], w, wsem)
        copy.start()
        acc[...] = jnp.zeros_like(acc)
        aq[...] = jnp.zeros_like(aq)
        ak[...] = jnp.zeros_like(ak)
        av[...] = jnp.zeros_like(av)
        gb_ref[...] = gb_in[...]
        copy.wait()

    rows, dk, dv = xs_ref[0], dk_ref[0], dv_ref[0]
    ak[...] += dot_tn(rows, dk)
    av[...] += dot_tn(rows, dv)
    gb_ref[1:2, :] += jnp.sum(dv.astype(F32), axis=0, keepdims=True)
    dx = dot_nt(dk, w[:, 48:96, :].reshape(768, 768)) + dot_nt(dv, w[:, 96:144, :].reshape(768, 768))

    def add(slot, off, n):
        start = pl.multiple_of(idx[m, slot], 64)
        acc[m, pl.ds(start, n), :] += dx[off:off + n]

    if not scattered:
        dx_ref[0] = jnp.where(i == 2, jnp.zeros_like(dx), dx).astype(BF)

    @pl.when((i < 5) & (i != 2) & scattered)
    def _():
        add(jnp.minimum(i, 4), 0, 256)

    @pl.when((i == 5) & scattered)
    def _():
        add(5, 0, 128)
        add(6, 128, 128)

    @pl.when((i > 5) & scattered)
    def _():
        for t in range(4):
            add(7 + 4 * (i - 6) + t, 64 * t, 64)

    @pl.when(i == 2)
    def _():
        dq = dq_ref[0]
        aq[...] += dot_tn(rows, dq)
        gb_ref[0:1, :] += jnp.sum(dq.astype(F32), axis=0, keepdims=True)
        own_ref[0] = dx + done_ref[0] + dot_nt(dq, w[:, 0:48, :].reshape(768, 768))

    @pl.when((i == CHUNKS - 1) & scattered)
    def _():
        dx_ref[m if scattered else 0] = acc[m].astype(BF)

    @pl.when((m == 1) & (i == CHUNKS - 1))
    def _():
        gq_ref[...] = aq[...].astype(BF)
        gk_ref[...] = ak[...].astype(BF)
        gv_ref[...] = av[...].astype(BF)


def back(idx, xs, dk, dv, dq, done, wall, gb, seq_len):
    mb = xs.shape[0]
    sd = jax.ShapeDtypeStruct
    chunk = pl.BlockSpec((1, 256, 768), lambda m, i, t: (m, i, 0))
    one = pl.BlockSpec((1, 256, 768), lambda m, i, t: (m, 0, 0))
    whole = lambda *s: pl.BlockSpec(s, lambda m, i, t: (0,) * len(s))
    scattered = seq_len > 0
    held = seq_len if scattered else 256
    return pl.pallas_call(
        functools.partial(back_kernel, scattered),
        grid_spec=pltpu.PrefetchScalarGridSpec(
            num_scalar_prefetch=1,
            grid=(mb, CHUNKS),
            in_specs=[chunk, chunk, chunk, one, one, pl.BlockSpec(memory_space=pl.ANY), whole(16, 768)],
            out_specs=[whole(mb, seq_len, 768) if scattered else chunk, one, whole(768, 768), whole(768, 768), whole(768, 768), whole(16, 768)],
            scratch_shapes=[
                pltpu.VMEM((16, 144, 768), BF), pltpu.SemaphoreType.DMA, pltpu.VMEM((mb, held, 768), F32),
                pltpu.VMEM((768, 768), F32), pltpu.VMEM((768, 768), F32), pltpu.VMEM((768, 768), F32),
            ],
        ),
        out_shape=[sd((mb, seq_len if scattered else NS, 768), BF), sd((mb, 256, 768), F32), sd((768, 768), BF), sd((768, 768), BF),
                   sd((768, 768), BF), sd((16, 768), F32)],
        compiler_params=pltpu.CompilerParams(vmem_limit_bytes=60 * 2**20),
    )(idx, xs, dk, dv, dq, done, wall, gb)


def last_kernel(*refs):
    table, arrays = refs[0], refs[1:8]
    outs, vectors = refs[8:15], refs[15:]
    for src, dst in zip(arrays, outs):
        dst[...] = src[...]
    owner = lax.axis_index("seq") * 4 + lax.axis_index("batch")
    n, m = vectors[0].shape[1], vectors[8].shape[1]
    small = pltpu.roll(table[0:8, :], (768 - owner * n) % 768, axis=1)
    for i in range(8):
        vectors[i][...] = small[i:i + 1, 0:n]
    ups = jnp.broadcast_to(table[pl.ds(8 + owner // 8, 1), :], (8, 768))
    vectors[8][...] = pltpu.roll(ups, (768 - (owner % 8) * m) % 768, axis=1)[0:1, 0:m]


def last(table, arrays, n, m):
    sd = jax.ShapeDtypeStruct
    vm = pl.BlockSpec(memory_space=pltpu.VMEM)
    return pl.pallas_call(
        last_kernel,
        in_specs=[vm] * 8,
        out_specs=[vm] * 16,
        out_shape=[sd(a.shape, a.dtype) for a in arrays] + [sd((1, n), F32)] * 8 + [sd((1, m), F32)],
        compiler_params=pltpu.CompilerParams(vmem_limit_bytes=32 * 2**20),
    )(table, *arrays)

def cat_rows(ref, h):
    return jnp.concatenate([ref[0, pl.ds(a, n), :] for a, n in key_rows(h)], axis=0)


def fwd_kernel(q_ref,k_ref,v_ref,me_ref,o_ref,l_ref):
    p=pl.program_id(1)
    ind=block_columns().astype(BF)
    for h in range(2):
        me=me_ref[0,h]
        qe=jnp.concatenate([split_heads(q_ref[0,pl.ds(h*HALF,HALF),:]),ind],axis=1)
        ke=jnp.concatenate([cat_rows(k_ref, h),me],axis=1)
        s=dot_nt(qe,ke)
        top=jnp.max(s,axis=1,keepdims=True)
        e=jnp.exp(s-top).astype(BF)
        ve=jnp.concatenate([cat_rows(v_ref,h),me],axis=1)
        o=dot(e,ve)
        tot=o[:,130:131]
        o_ref[0,pl.ds(h*HALF,HALF),:]=merge_heads(o[:,:128]/tot).astype(BF)
        l_ref[0,0,pl.ds(h*256,256),:]=jnp.broadcast_to(top+jnp.log(tot),(256,128))
def attn_fwd(q,k,v,me):
    mb=q.shape[0]; npair=q.shape[2]//128
    return pl.pallas_call(fwd_kernel,grid=(mb,npair),
      in_specs=[pl.BlockSpec((1,256,128),lambda m,p:(m,0,p)),pl.BlockSpec((1,NS,128),lambda m,p:(m,0,p)),pl.BlockSpec((1,NS,128),lambda m,p:(m,0,p)),
        pl.BlockSpec((1,2,NK,128),lambda m,p:(m,0,0,0))],
      out_specs=[pl.BlockSpec((1,256,128),lambda m,p:(m,0,p)),pl.BlockSpec((1,1,512,128),lambda m,p:(m,p,0,0))],
      out_shape=[jax.ShapeDtypeStruct(q.shape,BF),jax.ShapeDtypeStruct((mb,npair,512,128),F32)],
      compiler_params=pltpu.CompilerParams(vmem_limit_bytes=56*2**20))(q,k,v,me)
def bwd_kernel(CH,q_ref,k_ref,v_ref,me_ref,o_ref,do_ref,l_ref,dq_ref,dk_ref,dv_ref,dka,dva):
    ind=block_columns()
    zero=jnp.zeros_like(ind)
    dka[...]=jnp.zeros_like(dka); dva[...]=jnp.zeros_like(dva)
    for h in range(2):
        rows=pl.ds(h*HALF,HALF)
        qs=split_heads(q_ref[0,rows,:])
        do2=do_ref[0,rows,:]
        dos=split_heads(do2)
        o2=o_ref[0,rows,:].astype(F32)
        delta=jnp.sum(dos.astype(F32)*jnp.concatenate([o2,o2],axis=0),axis=1,keepdims=True)
        lse=l_ref[0,0,pl.ds(h*256,256),0:1]
        qe=jnp.concatenate([qs,with_column(ind,-lse)],axis=1)
        doe=jnp.concatenate([dos,with_column(zero,-delta)],axis=1)
        dqt=jnp.zeros((128,256),F32)
        off=0
        for a,n in key_rows(h):
            c0=0
            while c0<n:
                c=min(CH,n-c0)
                kr=pl.ds(a+c0,c)
                k2=k_ref[0,kr,:]; v2=v_ref[0,kr,:]; me=me_ref[0,h,pl.ds(off+c0,c),:]
                st=dot_nt(jnp.concatenate([k2,me],axis=1),qe)
                pt=jnp.exp(st)
                dpt=dot_nt(jnp.concatenate([v2,me],axis=1),doe)
                ds=(pt*dpt).astype(BF)
                dva[kr,:]+=dot(pt.astype(BF),dos)
                dka[kr,:]+=dot(ds,qs)
                dqt=dqt+dot(k2.T,ds)
                c0+=c
            off+=n
        dq_ref[0,rows,:]=(merge_heads(dqt.T)*0.125).astype(BF)
    dk_ref[0]=dka[...].astype(BF); dv_ref[0]=dva[...].astype(BF)
def attn_bwd(q,k,v,me,o,do,l,CH=384):
    mb=q.shape[0]; npair=q.shape[2]//128
    qs=pl.BlockSpec((1,256,128),lambda m,p:(m,0,p)); ks=pl.BlockSpec((1,NS,128),lambda m,p:(m,0,p))
    return pl.pallas_call(functools.partial(bwd_kernel,CH),grid=(mb,npair),
      in_specs=[qs,ks,ks,pl.BlockSpec((1,2,NK,128),lambda m,p:(m,0,0,0)),qs,qs,pl.BlockSpec((1,1,512,128),lambda m,p:(m,p,0,0))],
      out_specs=[qs,ks,ks],
      out_shape=[jax.ShapeDtypeStruct(q.shape,BF),jax.ShapeDtypeStruct(k.shape,BF),jax.ShapeDtypeStruct(k.shape,BF)],
      scratch_shapes=[pltpu.VMEM((NS,128),F32)]*2,
      compiler_params=pltpu.CompilerParams(vmem_limit_bytes=56*2**20))(q,k,v,me,o,do,l)


BLK = 64
WIN = 8
RAND = 3
ALL = ("seq", "batch")


def vector_table(vectors, b_up, owner, width):
    lane = jnp.arange(width, dtype=jnp.int32)
    n, m = vectors[0].shape[0], b_up.shape[0]
    table = jnp.where(lane // n == owner, jnp.tile(jnp.stack(vectors).astype(F32), (1, width // n)), 0.0)
    flat = jnp.arange(4 * width, dtype=jnp.int32)
    ups = jnp.where(flat // m == owner, jnp.tile(b_up.astype(F32), 4 * width // m), 0.0).reshape(4, width)
    return jnp.concatenate([table, ups, jnp.zeros((4, width), F32)], axis=0)


def block_plan(lengths, randoms, device, blocks):
    ends = jnp.cumsum(lengths, axis=1)
    starts = ends - lengths

    def doc_of(block):
        at = block * BLK
        shape = (lengths.shape[0],) + (1,) * (block.ndim - 1) + (lengths.shape[1],)
        doc = jnp.sum((ends.reshape(shape) <= at[..., None]).astype(jnp.int32), axis=-1)
        doc = jnp.minimum(doc, lengths.shape[1] - 1)
        hit = jnp.arange(lengths.shape[1], dtype=jnp.int32) == doc[..., None]
        return doc, jnp.sum(jnp.where(hit, starts.reshape(shape), 0), axis=-1)

    mb = lengths.shape[0]
    half = jnp.arange(2, dtype=jnp.int32)
    query = device * 4 + 2 * half[:, None] + half[None, :]
    query = jnp.broadcast_to(query[None], (mb, 2, 2))
    q_doc, q_first = doc_of(query)
    window = device * 4 + 2 * half[:, None] - WIN + jnp.arange(2 * WIN + 2, dtype=jnp.int32)[None, :]
    window = jnp.broadcast_to(window[None], (mb, 2, 2 * WIN + 2))
    w_doc, w_first = doc_of(jnp.clip(window, 0, blocks - 1))
    w_good = (window >= 0) & (window < blocks) & (window * BLK - w_first >= 2 * BLK)
    see_window = (
        w_good[:, :, None, :]
        & (w_doc[:, :, None, :] == q_doc[..., None])
        & (jnp.abs(window[:, :, None, :] - query[..., None]) <= WIN)
    )
    see_glob = jnp.ones((mb, 2, 2, 2), bool)
    named = lax.dynamic_slice_in_dim(randoms, device * 4, 4, 1).reshape(mb, 2, 2, RAND)
    r_doc, r_first = doc_of(named)
    r_good = (
        (r_doc == q_doc[..., None])
        & (jnp.abs(named - query[..., None]) > WIN)
        & (named * BLK - r_first >= 2 * BLK)
    )
    see_random = (r_good[:, :, None] & jnp.eye(2, dtype=bool)[None, None, :, :, None]).reshape(mb, 2, 2, 2 * RAND)
    see = jnp.concatenate([see_window, see_glob, see_random], axis=3)
    chunk = jnp.clip(device + jnp.arange(-2, 3, dtype=jnp.int32), 0, blocks // 4 - 1) * (4 * BLK)
    where = jnp.concatenate(
        [jnp.broadcast_to(chunk[None], (mb, 5)), q_first[:, :, 0], named.reshape(mb, -1) * BLK], axis=1
    )
    return where, jnp.where(see, 0.0, -1e30)


def mask_columns(see):
    bias = jnp.broadcast_to(see[..., None], see.shape + (BLK,)).reshape(see.shape[:3] + (-1, 1))
    lane = jnp.arange(128, dtype=jnp.int32)
    ones = jnp.where((lane >= 2) & (lane < 5), 1.0, 0.0)
    return jnp.where(lane == 0, bias[:, :, 0], jnp.where(lane == 1, bias[:, :, 1], ones)).astype(BF)


def on_device(inputs, cotangent, doc_lengths, random_blocks, wq, wk, wv, wo, wu, wd, b_query, b_value, b_out,
              b_up, b_down, gain_attn, bias_attn, gain_ffn, bias_ffn):
    mb, _, rows, width = inputs.shape
    devices, owners = lax.axis_size("seq"), lax.axis_size("seq") * lax.axis_size("batch")
    device = lax.axis_index("seq")
    owner = device * lax.axis_size("batch") + lax.axis_index("batch")
    linked = devices == 8 and owners == 32
    seq_len = devices * rows
    x, cot = inputs[:, 0], cotangent[:, 0]
    lengths, randoms = doc_lengths[:, 0], random_blocks[:, 0]
    vectors = (b_query, b_value, b_out, b_down, gain_attn, bias_attn, gain_ffn, bias_ffn)
    flat = lambda t: t.reshape(-1, t.shape[-1])
    if linked:
        att, lse, q, xs, k, v, wall, top, bias, extra, targets = forward_all(
            lengths, randoms, x, (wq, wk, wv, wo, wu, wd), jnp.stack(vectors), b_up[None])
    else:
        where, see = block_plan(lengths, randoms, device, seq_len // BLK)
        extra, table = mask_columns(see), vector_table(vectors, b_up, owner, width)
        xall = lax.all_gather(x, "seq", axis=1, tiled=True)
        bias = lax.psum(table, ALL)
        full = [lax.all_gather(w, ALL, axis=0, tiled=True) for w in (wq, wk, wv, wo, wu, wd)]
        fold = lambda w: w.reshape(16, -1, width)
        up = full[4].reshape(16, 48, 4, width).transpose(0, 2, 1, 3).reshape(16, 192, width)
        wall = jnp.concatenate([fold(full[3]), up, fold(full[5])], axis=1)
        top = jnp.concatenate([jnp.zeros((16, 16, width), BF)] + [fold(w) for w in full[:3]], axis=1)
        xs, k, v, q = project(where, xall, top, bias)
        att, lse = attn_fwd(q, k, v, extra)
    stats = flat(lse) if linked else jnp.zeros((mb * rows, 128), F32)
    out, stats, datt, done, go, gu, gd, gb = middle(flat(att), flat(x), flat(cot), wall, bias, stats)
    datt, done = datt.reshape(att.shape), done.reshape(mb, rows, width)
    if linked:
        *grads, gb, dx = backward_all(datt, stats.reshape(mb, rows, 128), targets, gb, extra, q, done, k, v, xs, top, go, gu, gd)
    else:
        dq, dk, dv = attn_bwd(q, k, v, extra, att, datt, lse, 640)
        dxs, own, gq, gk, gv, gb = back(where, xs, dk, dv, dq, done, top, gb, 0)
        start = (where[:, :5, None] + jnp.arange(0, 256, BLK)).reshape(mb, -1)
        glob = (where[:, 5:7, None] + jnp.arange(0, 128, BLK)).reshape(mb, -1)
        to = jnp.concatenate([start, glob, where[:, 7:]], axis=1) // BLK
        parts = dxs.reshape(mb, -1, BLK, width)
        total = jnp.zeros((mb, seq_len // BLK, BLK, width), F32)
        total = jax.vmap(lambda t, i, p: t.at[i].add(p))(total, to, parts.astype(F32))
        dx = own + lax.psum_scatter(total.reshape(mb, seq_len, width), "seq", scatter_dimension=1, tiled=True)
        grads = [lax.psum_scatter(g.astype(F32), ALL, scatter_dimension=0, tiled=True) for g in (gq, gk, gv, go, gu, gd)]
        gb = lax.psum(gb, ALL)
    n, m = b_query.shape[0], b_up.shape[0]
    if linked:
        done_all = last(gb, (*grads, dx), n, m)
        grads, dx = done_all[:6], done_all[6]
        small, ups = [g.reshape(n) for g in done_all[7:15]], done_all[15].reshape(m)
    else:
        small = lax.dynamic_slice_in_dim(gb[:8], owner * n, n, 1)
        ups = lax.dynamic_slice_in_dim(gb[8:12].reshape(-1), owner * m, m, 0)
    return (
        out.reshape(inputs.shape), dx[:, None], *grads,
        small[0], small[1], small[2], ups, small[3], small[4], small[5], small[6], small[7],
    )


def solution(mesh):
    tokens = P(None, "batch", "seq", None)
    mat, vec = P(ALL, None), P(ALL)
    in_specs = (tokens, tokens, P(None, "batch", None), P(None, "batch", None, None)) + (mat,) * 6 + (vec,) * 9
    out_specs = (tokens, tokens) + (mat,) * 6 + (vec,) * 9
    return jax.shard_map(on_device, mesh=mesh, in_specs=in_specs, out_specs=out_specs, check_vma=False)
```

profile of v0, /device:TPU:0, one launch (start us, length us, event | category | flops | bytes accessed | tf_op | source)
XLA Modules:
  0.0 327.9 jit_solution(2531237028192112785)
XLA Ops:
  0.7 1.4 stack.35.vectors
  2.0 1.4 copy.36
  3.4 132.0 %shard_map.314 = (bf16[2,256,768]{2,1,0:T(8,128)(2,1)}, f32[2,256,128]{2,1,0:T(8,128)}, bf16[2,256,768]{2,1,0:T(8,128)(2,1)}, bf16[2,2304,768]{2,1,0:T(8,128)(2,...) custom-call(s32[2,4]{1,0:T(2,128)} %bitcast.51, ...), custom_call_target="tpu_custom_call" | custom-call | tf_op jit(solution)/shard_map/pallas_call | solution.py:497
  135.4 32.1 %shard_map.315 = (bf16[512,768]{1,0:T(8,128)(2,1)}, f32[512,128]{1,0:T(8,128)}, bf16[512,768]{1,0:T(8,128)(2,1)}, f32[512,768]{1,0:T(8,128)}, bf16[768,768]{1,0:...) custom-call(bf16[512,768]{1,0:T(8,128)(2,1)} %bitcast.46, ...), custom_call_target="tpu_custom_call" | custom-call | tf_op jit(solution)/shard_map/pallas_call | solution.py:1241
  167.5 151.0 %shard_map.316 = (f32[24,768]{1,0:T(8,128)}, f32[24,768]{1,0:T(8,128)}, f32[24,768]{1,0:T(8,128)}, f32[24,768]{1,0:T(8,128)}, f32[24,3072]{1,0:T(8,128)}, /*inde...) custom-call(bf16[2,256,768]{2,1,0:T(8,128)(2,1)} %bitcast.47, f32[2,256,128]{2,1,0:T(8,128)} %bitcast.48, ...), custom_call_target="tpu_custom_call" | custom-call | tf_op jit(solution)/shard_map/pallas_call | solution.py:1032
  318.5 0.0 copy-start
  318.5 1.4 copy-done
  319.9 0.0 copy-start.1
  319.9 1.0 copy-done.1
  320.9 0.0 copy-start.2
  320.9 1.0 copy-done.2
  321.9 0.0 copy-start.3
  321.9 0.9 copy-done.3
  322.7 0.0 copy-start.4
  322.7 0.9 copy-done.4
  323.6 0.0 copy-start.5
  323.6 0.9 copy-done.5
  324.5 0.0 copy-start.6
  324.5 0.9 copy-done.6
  325.4 0.0 copy-start.7
  325.4 0.8 copy-done.7
  326.2 1.5 shard_map.317
Async XLA Ops:
  318.5 1.4 copy-start
  319.9 1.0 copy-start.1
  320.9 1.0 copy-start.2
  321.9 0.9 copy-start.3
  322.7 0.9 copy-start.4
  323.6 0.9 copy-start.5
  324.5 0.9 copy-start.6
  325.4 0.8 copy-start.7
where the time goes:
time: 328 us
  Pallas kernels  317 us (97%)
  local copies, waits for them, and re-layouts  10.4 us (3%)
    pallas_call x1, Pallas kernels, backward_all(): pl.pallas_call(backward_kernel, out_shape=[sd((24, width), F32)] * 4 + [s...  151 us
    pallas_call x1, Pallas kernels, forward_all(): pl.pallas_call(forward_kernel, out_shape=[sd((mb, rows, width), BF), sd((...  132 us
    pallas_call x1, Pallas kernels, middle(): pl.pallas_call(middle_kernel, in_specs=[vm, vm, vm, pl.BlockSpec(memory_s...  32.1 us
    unnamed x17, local copies, waits for them, and re-layouts  9.04 us

commit v1 on v0

--- a/solution.py
+++ b/solution.py
@@ -102,7 +102,7 @@
     at = block * 64
     doc, first, end = jnp.int32(0), jnp.int32(0), jnp.int32(0)
     for i in range(3):
-        end = end + lengths[m, i]
+        end = end + lengths[m, 0, i]
         doc = doc + (end <= at).astype(jnp.int32)
         first = jnp.where(end <= at, end, first)
     return doc, first
@@ -115,7 +115,7 @@
     def one(i, _):
         m, h, t = i // 52, (i // 26) % 2, i % 26
         r = jnp.maximum(t - 20, 0)
-        named = randoms[m, 4 * s + 2 * h + r // 3, r % 3]
+        named = randoms[m, 0, 4 * s + 2 * h + r // 3, r % 3]
         block = jnp.where(t < 18, 4 * s + 2 * h - 8 + t, named)
         inside = (block >= 0) & (block < 32)
         doc, first = doc_of(lengths, m, jnp.clip(block, 0, 31))
@@ -138,7 +138,7 @@
 
 def rest_block(lengths, randoms, s, m, t):
     r = jnp.maximum(t - 4, 0)
-    named = randoms[m, 4 * s + r // 3, r % 3]
+    named = randoms[m, 0, 4 * s + r // 3, r % 3]
     _, first = doc_of(lengths, m, 4 * s + 2 * jnp.minimum(t // 2, 1))
     return jnp.where(t < 4, first // 64 + t % 2, named)
 
@@ -217,8 +217,6 @@
     for i in range(5):
         merged_b[48 * i:48 * i + 48, :] = paired(88 + 24 * i, 24)
     merged_b[240:432, :] = paired(208, 96)
-    b_copy(z, x, y, YY, merged_b).start()
-    b_copy(z, x, y, CC, merged_b).start()
     keep_b = pltpu.make_async_copy(merged_b, wall.at[s * 2 + y, :, mine], lsem.at[3])
     keep_b.start()
     write_extra(lengths, randoms, s, extra)
@@ -323,30 +321,18 @@
         pl.when(k == 0)(first)
         pl.when((k > 0) & (k <= 3))(later)
 
-    def start_x1(way):
-        guarded(way, lambda: x_copy(1, z, x, way, True).start())
-
-    def start_relay(k, _):
-        x_line(0, k)
-        w_line(a_copy, k)
-        w_from_x(a_copy, k - 1)
-
-        @pl.when(k == 2)
-        def _():
-            start_x1(UP)
-            start_x1(DOWN)
-            for way in (UP, DOWN):
-                guarded(way, lambda way=way: b_copy(z, x, y, way, merged_b).start())
-
-        return 0
-
-    lax.fori_loop(1, 4, start_relay, 0)
-    start_x1(XX)
-    w_from_x(a_copy, 3)
-    x_line(1, 1)
-    b_copy(z, x, y, XX, merged_b).start()
-    for xx in (x, 1 - x):
-        lax.fori_loop(0, 4, lambda k, _, xx=xx: (w_from_y(a_copy, xx, k), 0)[1], 0)
+    begin = {
+        "x0": lambda k: x_line(0, k),
+        "x1": lambda k: x_line(1, k),
+        "a": lambda k: w_line(a_copy, k),
+        "ax": lambda k: w_from_x(a_copy, k),
+        "ay0": lambda k: w_from_y(a_copy, x, k),
+        "ay1": lambda k: w_from_y(a_copy, 1 - x, k),
+        "own x1": lambda ways: [guarded(way, lambda way=way: x_copy(1, z, x, way, True).start()) for way in ways],
+        "own b": lambda ways: [guarded(way, lambda way=way: b_copy(z, x, y, way, merged_b).start()) for way in ways],
+    }
+    for name, what in START:
+        begin[name](what)
     keep_a.wait()
 
     def arrived(i, _):
@@ -366,16 +352,25 @@
         src, dst = ((xs, xs_out), (ks, k_out), (vs, v_out))[t]
         return pltpu.make_async_copy(src.at[m], dst.at[m], osem.at[m, t])
 
-    def gather(m):
-        def x_here(zz):
+    def x_here(m, k):
+        def arrived_x(zz):
             x_copy(m, zz, 1 - x, XX).wait_recv()
 
-        for k in range(4):
-            at_distance(x_here, k)
+        at_distance(arrived_x, k)
+
+    def gather_near(m):
+        x_here(m, 0)
+        x_here(m, 1)
         pltpu.make_async_copy(x_ref.at[m], xall[m].at[pl.ds(4 * s, 4)], lsem.at[m]).wait()
         for t in range(5):
             chunk = xall[m][pl.ds(4 * jnp.clip(s - 2 + t, 0, 7), 4)]
             xs[m, 256 * t:256 * t + 256, :] = chunk.reshape(256, chunk.shape[-1])
+        q = (dot(xs[m, 512:768, :], wa[:, 16:64, :].reshape(768, 768)) + bias[0:1, :]).astype(BF)
+        q_out[m] = q * jnp.asarray(0.125, BF)
+
+    def gather_rest(m):
+        x_here(m, 2)
+        x_here(m, 3)
 
         def named(t, _):
             xs[m, pl.ds(pl.multiple_of(NW + 64 * t, 64), 64), :] = xall[m][rest_block(lengths, randoms, s, m, t)]
@@ -383,11 +378,8 @@
 
         lax.fori_loop(0, 16, named, 0)
         out_copy(m, 0).start()
-        q = (dot(xs[m, 512:768, :], wa[:, 16:64, :].reshape(768, 768)) + bias[0:1, :]).astype(BF)
-        q_out[m] = q * jnp.asarray(0.125, BF)
-
-    def project(m, i):
-        r = rows_at(i, 768)
+
+    def project(m, r):
         rows = xs[m, r, :]
         ks[m, r, :] = dot(rows, wa[:, 64:112, :].reshape(768, 768)).astype(BF)
         vs[m, r, :] = (dot(rows, wa[:, 112:160, :].reshape(768, 768)) + bias[1:2, :]).astype(BF)
@@ -416,18 +408,21 @@
         return k
 
     def pump(g):
-        x_line(1, picked(g, PUMP_X))
-        b_own_column(picked(g, PUMP_OWN))
-        b_other_column(picked(g, PUMP_OTHER))
-        b_to_x(picked(g, PUMP_CROSS))
-        w_from_y(b_copy, x, picked(g, PUMP_Y0))
-        w_from_y(b_copy, 1 - x, picked(g, PUMP_Y1))
+        for name in PUMP_ORDER:
+            k = picked(g, PUMPS[name])
+            act = {
+                "x1": lambda k: x_line(1, k), "bo": b_own_column, "bt": b_other_column, "bc": b_to_x,
+                "by0": lambda k: w_from_y(b_copy, x, k), "by1": lambda k: w_from_y(b_copy, 1 - x, k),
+            }[name]
+            act(k)
 
     def step(g, _):
         m, i = g // 9, g % 9
-        pl.when(g == 0)(lambda: gather(0))
-        pl.when(g == 9)(lambda: gather(1))
-        pl.when(i < 3)(lambda: project(m, i))
+        for mm in range(2):
+            pl.when(g == 9 * mm)(lambda mm=mm: gather_near(mm))
+            pl.when(g == 9 * mm + 2)(lambda mm=mm: gather_rest(mm))
+        pl.when(i < 2)(lambda: project(m, rows_at(jnp.minimum(i, 1), 640)))
+        pl.when(i == 2)(lambda: project(m, pl.ds(NW, NS - NW)))
 
         @pl.when(i == 3)
         def _():
@@ -440,7 +435,7 @@
 
     lax.fori_loop(0, 18, step, 0)
 
-    lax.fori_loop(18, 26, lambda g, _: (pump(g), 0)[1], 0)
+    lax.fori_loop(18, 24, lambda g, _: (pump(g), 0)[1], 0)
 
     def b_arrived(i, _):
         ref = wall.at[i, :, theirs]
@@ -480,12 +475,41 @@
     lax.fori_loop(0, 4, sent, 0)
 
 
-PUMP_X = ((1, 2), (6, 3))
-PUMP_OWN = ((0, 1), (4, 2), (8, 3))
-PUMP_OTHER = ((3, 0), (8, 1), (12, 2), (15, 3))
-PUMP_CROSS = ((6, 1), (8, 2), (9, 3))
-PUMP_Y0 = ((1, 0), (3, 1), (7, 2), (10, 3))
-PUMP_Y1 = ((7, 0), (12, 1), (15, 2), (18, 3))
+START = (
+    ("x0", 1),
+    ("a", 1),
+    ("ay0", 0),
+    ("ax", 0),
+    ("a", 2),
+    ("a", 3),
+    ("x0", 2),
+    ("own x1", (UP, DOWN,)),
+    ("ax", 2),
+    ("ax", 1),
+    ("x0", 3),
+    ("ay0", 1),
+    ("ay0", 3),
+    ("ay1", 2),
+    ("own b", (UP, DOWN,)),
+    ("ax", 3),
+    ("ay1", 3),
+    ("ay0", 2),
+    ("ay1", 0),
+    ("own b", (XX,)),
+    ("own x1", (XX,)),
+    ("ay1", 1),
+    ("own b", (YY, CC,)),
+    ("x1", 1),
+)
+PUMP_ORDER = ("x1", "bo", "bc", "bt", "by0", "by1")
+PUMPS = {
+    "x1": ((2, 2), (9, 3),),
+    "bo": ((0, 1), (5, 2), (10, 3),),
+    "bt": ((2, 0), (9, 1), (11, 2), (14, 3),),
+    "bc": ((0, 1), (9, 2), (11, 3),),
+    "by0": ((2, 0), (5, 1), (11, 2), (15, 3),),
+    "by1": ((9, 0), (13, 1), (14, 2), (16, 3),),
+}
 
 
 def forward_all(lengths, randoms, x, weights, vectors, b_up):
@@ -841,28 +865,70 @@
     swap2 = [remote(ga.at[:, yy, :, theirs], mate2.at[:, yy], msem2.at[0, t], msem2.at[1, t], near_c)
              for t, yy in enumerate((1 - y, y))]
 
+    def rest_rows(cc):
+        yield oo, 0, pl.multiple_of(24 * cc, 8), 24, 0
+        for j in range(4):
+            yield ou, 24 + 24 * j, pl.multiple_of(48 + 48 * j + 24 * cc, 8), 24, 768 * j
+        yield od, 120, pl.multiple_of(240 + 96 * cc, 8), 96, 0
+
+    def top_rows(cc):
+        yield ob, 216, 0, 16, 0
+        for i, ref in enumerate((oq, ok, ov)):
+            yield ref, 232 + 24 * i, pl.multiple_of(16 + 48 * i + 24 * cc, 8), 24, 0
+
+    def to_mate(rows_of, first):
+        return [remote(fin.at[pl.ds(start, n), :], rcv.at[at:at + n, :], fsem.at[0, first + i], fsem.at[1, first + i], near_c)
+                for i, (_, at, start, n, _) in enumerate(rows_of(1 - c))]
+
+    def hand_over(rows_of):
+        for ref, at, start, n, col in rows_of(c):
+            ref[:, pl.ds(pl.multiple_of(col + c * 384, 128), 384)] = fin[pl.ds(start, n), :]
+
+    def take_over(rows_of):
+        for ref, at, start, n, col in rows_of(c):
+            ref[:, pl.ds(pl.multiple_of(col + (1 - c) * 384, 128), 384)] = rcv[at:at + n, :]
+
+    last0 = to_mate(rest_rows, 0)
+
     def picked(g, plan):
         k = jnp.full((), 9, jnp.int32)
         for at, value in plan:
             k = jnp.where(g == at, value, k)
         return k
 
-    def pump(g):
-        k = picked(g, PLAN_Y)
-        pl.when(k < 9)(lambda: rest.y_step(k))
-        k2 = picked(g, PLAN_X)
-        pl.when(k2 < 9)(lambda: rest.x_step(k2))
-        k3 = picked(g, PLAN_D)
-        pl.when(k3 < 3)(lambda: dx_step(0, k3))
-        k4 = picked(g, PLAN_Z)
-        pl.when(k4 < 3)(lambda: rest.z_step(k4))
-
-        def start_top():
-            swap2[0].wait_recv()
-            swap2[1].wait_recv()
-            lax.fori_loop(0, 8, lambda i, _: (top.y_step(i), 0)[1], 0)
-
-        pl.when(g == PLAN_TOP)(start_top)
+    def start_top(_):
+        swap2[0].wait_recv()
+        swap2[1].wait_recv()
+        lax.fori_loop(0, 8, lambda i, _: (top.y_step(i), 0)[1], 0)
+
+    def tell(to):
+        pl.semaphore_signal(ready, inc=1, device_id=to, device_id_type=MESH)
+
+    def end_rest(_):
+        rest.finish()
+        for to in (near_x, near_y, near_c):
+            tell(to)
+        pl.when(z > 0)(lambda: tell(below))
+        pl.when(z < 3)(lambda: tell(above))
+        for cp in last0:
+            cp.start()
+        hand_over(rest_rows)
+
+    def all_ready(_):
+        pl.semaphore_wait(ready, 3 + (z > 0).astype(jnp.int32) + (z < 3).astype(jnp.int32))
+
+    acts = {
+        "Y": rest.y_step, "X": rest.x_step, "Z": rest.z_step, "BF": end_rest, "W": all_ready,
+        "D0": functools.partial(dx_step, 0), "D0F": lambda _: dx_finish(0), "D1": functools.partial(dx_step, 1),
+        "TY": start_top, "TX": top.x_step, "TZ": top.z_step,
+    }
+
+    def pump(g, first, last_):
+        for name in STEP_ORDER:
+            plan = [(at, k) for at, k in STEPS[name] if first <= at < last_]
+            if plan:
+                k = picked(g, plan)
+                pl.when(k < 9)(lambda name=name, k=k: acts[name](k))
 
     for i in range(6):
         loads[0, i].wait()
@@ -878,111 +944,49 @@
     def micro(m, _):
         load_xs(m).start()
 
-        def pairs(p, _):
-            pair(m, p)
-
-            @pl.when((m == 0) & (p == 4))
+        def one(i, _):
+            @pl.when(i < 6)
             def _():
-                for i in range(6):
-                    loads[1, i].wait()
-                    swaps[1, i].wait_recv()
+                pair(m, jnp.minimum(i, 5))
+
+            @pl.when((m == 0) & (i == MATE_AT))
+            def _():
+                for t in range(6):
+                    loads[1, t].wait()
+                    swaps[1, t].wait_recv()
                 top_copy.wait()
 
-            pump(12 * m + p)
+            pl.when(i == 6)(lambda: load_xs(m).wait())
+            pl.when((i >= 6) & (i < 8))(lambda: weight_grads(m, jnp.clip(i - 6, 0, 1)))
+
+            @pl.when(i == 8)
+            def _():
+                gb[0:1, :] += jnp.sum(q[m].astype(F32), axis=0, keepdims=True)
+
+                def value_bias(t, _):
+                    gb[1:2, :] += jnp.sum(vb[rows_at(t, 256), :].astype(F32), axis=0, keepdims=True)
+                    return 0
+
+                lax.fori_loop(0, 9, value_bias, 0)
+
+            pl.when(i >= 9)(lambda: dx_rows(m, jnp.clip(i - 9, 0, 2)))
+            pump(12 * m + i, 0, 24)
+
+            @pl.when((m == 1) & (i == 8))
+            def _():
+                small_grads()
+                for cp in swap2:
+                    cp.start()
+
             return 0
 
-        lax.fori_loop(0, 6, pairs, 0)
-        load_xs(m).wait()
-
-        def grads(i, _):
-            weight_grads(m, i)
-            pump(12 * m + 6 + i)
-            return 0
-
-        lax.fori_loop(0, 2, grads, 0)
-        gb[0:1, :] += jnp.sum(q[m].astype(F32), axis=0, keepdims=True)
-
-        def value_bias(i, _):
-            gb[1:2, :] += jnp.sum(vb[rows_at(i, 256), :].astype(F32), axis=0, keepdims=True)
-            return 0
-
-        lax.fori_loop(0, 9, value_bias, 0)
-        pump(12 * m + 8)
-
-        @pl.when(m == 1)
-        def _():
-            small_grads()
-            for cp in swap2:
-                cp.start()
-
-        def rows(i, _):
-            dx_rows(m, i)
-            pump(12 * m + 9 + i)
-            return 0
-
-        lax.fori_loop(0, 3, rows, 0)
+        lax.fori_loop(0, 12, one, 0)
         pl.when(m == 0)(lambda: start_keys(1))
         lax.fori_loop(0, 8, lambda i, _: (dx_piece(m, i), 0)[1], 0)
         return 0
 
     lax.fori_loop(0, 2, micro, 0)
-
-    def rest_rows(cc):
-        yield oo, 0, pl.multiple_of(24 * cc, 8), 24, 0
-        for j in range(4):
-            yield ou, 24 + 24 * j, pl.multiple_of(48 + 48 * j + 24 * cc, 8), 24, 768 * j
-        yield od, 120, pl.multiple_of(240 + 96 * cc, 8), 96, 0
-
-    def top_rows(cc):
-        yield ob, 216, 0, 16, 0
-        for i, ref in enumerate((oq, ok, ov)):
-            yield ref, 232 + 24 * i, pl.multiple_of(16 + 48 * i + 24 * cc, 8), 24, 0
-
-    def to_mate(rows_of, first):
-        return [remote(fin.at[pl.ds(start, n), :], rcv.at[at:at + n, :], fsem.at[0, first + i], fsem.at[1, first + i], near_c)
-                for i, (_, at, start, n, _) in enumerate(rows_of(1 - c))]
-
-    def hand_over(rows_of):
-        for ref, at, start, n, col in rows_of(c):
-            ref[:, pl.ds(pl.multiple_of(col + c * 384, 128), 384)] = fin[pl.ds(start, n), :]
-
-    def take_over(rows_of):
-        for ref, at, start, n, col in rows_of(c):
-            ref[:, pl.ds(pl.multiple_of(col + (1 - c) * 384, 128), 384)] = rcv[at:at + n, :]
-
-    def tell(to):
-        pl.semaphore_signal(ready, inc=1, device_id=to, device_id_type=MESH)
-
-    last0 = to_mate(rest_rows, 0)
-
-    def tail(g, _):
-        def step(plan, act):
-            k = picked(g, plan)
-            pl.when(k < 9)(lambda: act(k))
-
-        @pl.when(g == TAIL_B)
-        def _():
-            rest.finish()
-            for to in (near_x, near_y, near_c):
-                tell(to)
-            pl.when(z > 0)(lambda: tell(below))
-            pl.when(z < 3)(lambda: tell(above))
-            for cp in last0:
-                cp.start()
-            hand_over(rest_rows)
-
-        @pl.when(g == TAIL_W)
-        def _():
-            pl.semaphore_wait(ready, 3 + (z > 0).astype(jnp.int32) + (z < 3).astype(jnp.int32))
-
-        step(TAIL_D0, lambda k: dx_step(0, k))
-        pl.when(g == TAIL_D0_END)(lambda: dx_finish(0))
-        step(TAIL_X, top.x_step)
-        step(TAIL_D, lambda k: dx_step(1, k))
-        step(TAIL_Z, top.z_step)
-        return 0
-
-    lax.fori_loop(0, TAIL, tail, 0)
+    lax.fori_loop(24, 38, lambda g, _: (pump(g, 24, 38), 0)[1], 0)
     dx_finish(1)
     for cp in last0:
         cp.wait()
@@ -1006,19 +1010,21 @@
         cp.wait_send()
 
 
-PLAN_Y = ((0, 1), (1, 2), (2, 3), (3, 4), (4, 5), (5, 6), (6, 7))
-PLAN_X = ((5, 0), (6, 1), (8, 2), (11, 3))
-PLAN_Z = ((13, 0), (16, 1), (19, 2))
-PLAN_D = ((16, 0), (20, 1), (23, 2))
-PLAN_TOP = 21
-TAIL_B = 0
-TAIL_W = 1
-TAIL_D0 = ()
-TAIL_D0_END = 1
-TAIL_X = ((1, 0), (2, 1), (3, 2), (4, 3))
-TAIL_D = ((1, 0), (3, 1), (5, 2))
-TAIL_Z = ((4, 0), (5, 1), (6, 2))
-TAIL = 7
+STEP_ORDER = ("X", "TY", "W", "D1", "BF", "Y", "D0", "TX", "TZ", "D0F", "Z")
+STEPS = {
+    "Y": ((1, 1), (2, 2), (3, 3), (5, 4), (7, 5), (9, 6), (24, 7),),
+    "X": ((2, 0), (3, 1), (5, 2), (8, 3),),
+    "Z": ((11, 0), (12, 1), (20, 2),),
+    "D0": ((14, 0), (18, 1), (23, 2),),
+    "TY": ((29, 0),),
+    "BF": ((29, 0),),
+    "W": ((32, 0),),
+    "D0F": ((24, 0),),
+    "TX": ((32, 0), (33, 1), (35, 2), (37, 3),),
+    "D1": ((27, 0), (29, 1), (32, 2),),
+    "TZ": ((33, 0), (35, 1), (37, 2),),
+}
+MATE_AT = 2
 
 
 def backward_all(datt, stats, tgt, gb, extra, q, done, k, v, xs, top, go, gu, gd):
@@ -1161,8 +1167,11 @@
         for h in range(2):
             r = pl.ds(h * half, half)
             u = dot(low[r, :], wu) + bias[pl.ds(8 + j, 1), :]
-            pre[j, r, :] = u
-            g = (0.5 * u * (1.0 + jnp.tanh(G0 * (u + G1 * u * u * u)))).astype(BF)
+            square = u * u
+            th = jnp.tanh(G0 * u * (1.0 + G1 * square))
+            half_u, one = 0.5 * u, 1.0 + th
+            pre[j, r, :] = 0.5 * one + half_u * (one * (1.0 - th)) * (G0 + (3.0 * G0 * G1) * square)
+            g = (half_u * one).astype(BF)
             hid[j, r, :] = g
             ffn[r, :] += dot(g, wd)
         return 0
@@ -1193,10 +1202,7 @@
         sent(gd_ref, gd_out, j, 0).start()
         for h in range(2):
             r = pl.ds(h * half, half)
-            u = pre[j, r, :]
-            th = jnp.tanh(G0 * (u + G1 * u * u * u))
-            slope = 0.5 * (1.0 + th) + 0.5 * u * (1.0 - th * th) * (G0 * (1.0 + 3.0 * G1 * u * u))
-            d_pre = (dot_nt(datt_ref[r, :], wd) * slope).astype(BF)
+            d_pre = (dot_nt(datt_ref[r, :], wd) * pre[j, r, :]).astype(BF)
             hid[j, r, :] = d_pre
             gb_ref[pl.ds(8 + j, 1), :] += jnp.sum(d_pre.astype(F32), axis=0, keepdims=True)
             mid[r, :] += dot_nt(d_pre, wu)
@@ -1364,7 +1370,7 @@
         in_specs=[vm] * 8,
         out_specs=[vm] * 16,
         out_shape=[sd(a.shape, a.dtype) for a in arrays] + [sd((1, n), F32)] * 8 + [sd((1, m), F32)],
-        compiler_params=pltpu.CompilerParams(vmem_limit_bytes=32 * 2**20),
+        compiler_params=pltpu.CompilerParams(vmem_limit_bytes=60 * 2**20),
     )(table, *arrays)
 
 def cat_rows(ref, h):
@@ -1517,7 +1523,7 @@
     flat = lambda t: t.reshape(-1, t.shape[-1])
     if linked:
         att, lse, q, xs, k, v, wall, top, bias, extra, targets = forward_all(
-            lengths, randoms, x, (wq, wk, wv, wo, wu, wd), jnp.stack(vectors), b_up[None])
+            doc_lengths, random_blocks, x, (wq, wk, wv, wo, wu, wd), jnp.stack(vectors), b_up[None])
     else:
         where, see = block_plan(lengths, randoms, device, seq_len // BLK)
         extra, table = mask_columns(see), vector_table(vectors, b_up, owner, width)

time: 328 us -> 311 us (0.948)
  Pallas kernels: 317 us -> 307 us
  local copies, waits for them, and re-layouts: 10.4 us -> 2.75 us
    unnamed x17 -> x1, local copies, waits for them, and re-layouts: 9.04 us -> 1.39 us
    pallas_call x1, Pallas kernels: 132 us -> 125 us  [forward_all(): pl.pallas_call(forward_kernel, out_shape=[sd((mb, rows, width), BF), sd((...]
    pallas_call x1, Pallas kernels: 151 us -> 148 us  [backward_all(): pl.pallas_call(backward_kernel, out_shape=[sd((24, width), F32)] * 4 + [s...]
where the time goes in v1:
time: 311 us
  Pallas kernels  307 us (99%)
    pallas_call x1, Pallas kernels, backward_all(): pl.pallas_call(backward_kernel, out_shape=[sd((24, width), F32)] * 4 + [s...  148 us
    pallas_call x1, Pallas kernels, forward_all(): pl.pallas_call(forward_kernel, out_shape=[sd((mb, rows, width), BF), sd((...  125 us
    pallas_call x1, Pallas kernels, middle(): pl.pallas_call(middle_kernel, in_specs=[vm, vm, vm, pl.BlockSpec(memory_s...  31.7 us

profile of v1, /device:TPU:0, one launch (start us, length us, event | category | flops | bytes accessed | tf_op | source)
XLA Modules:
  0.0 310.8 jit_solution(2717990150663369181)
XLA Ops:
  0.7 1.4 stack.35.vectors
  2.0 1.4 copy.36.randoms
  3.4 124.7 %shard_map.314 = (bf16[2,256,768]{2,1,0:T(8,128)(2,1)}, f32[2,256,128]{2,1,0:T(8,128)}, bf16[2,256,768]{2,1,0:T(8,128)(2,1)}, bf16[2,2304,768]{2,1,0:T(8,128)(2,...) custom-call(s32[2,1,4]{2,1,0:T(1,128)} %lengths.1, ...), custom_call_target="tpu_custom_call" | custom-call | tf_op jit(solution)/shard_map/pallas_call | solution.py:521
  128.1 31.7 %shard_map.315 = (bf16[512,768]{1,0:T(8,128)(2,1)}, f32[512,128]{1,0:T(8,128)}, bf16[512,768]{1,0:T(8,128)(2,1)}, f32[512,768]{1,0:T(8,128)}, bf16[768,768]{1,0:...) custom-call(bf16[512,768]{1,0:T(8,128)(2,1)} %bitcast.44, ...), custom_call_target="tpu_custom_call" | custom-call | tf_op jit(solution)/shard_map/pallas_call | solution.py:1247
  159.8 147.6 %shard_map.316 = (f32[24,768]{1,0:T(8,128)}, f32[24,768]{1,0:T(8,128)}, f32[24,768]{1,0:T(8,128)}, f32[24,768]{1,0:T(8,128)}, f32[24,3072]{1,0:T(8,128)}, /*inde...) custom-call(bf16[2,256,768]{2,1,0:T(8,128)(2,1)} %bitcast.45, f32[2,256,128]{2,1,0:T(8,128)} %bitcast.46, ...), custom_call_target="tpu_custom_call" | custom-call | tf_op jit(solution)/shard_map/pallas_call | solution.py:1038
  307.4 3.3 %shard_map.317 = (f32[24,768]{1,0:T(8,128)}, f32[24,768]{1,0:T(8,128)}, f32[24,768]{1,0:T(8,128)}, f32[24,768]{1,0:T(8,128)}, f32[24,3072]{1,0:T(8,128)}, /*inde...) custom-call(f32[16,768]{1,0:T(8,128)} %get-tuple-element.79.refs_0_,, ...), custom_call_target="tpu_custom_call" | custom-call | tf_op jit(solution)/shard_map/pallas_call | solution.py:1368

commit v2 on v1

--- a/solution.py
+++ b/solution.py
@@ -102,7 +102,7 @@
     at = block * 64
     doc, first, end = jnp.int32(0), jnp.int32(0), jnp.int32(0)
     for i in range(3):
-        end = end + lengths[m, 0, i]
+        end = end + lengths[0, m, i]
         doc = doc + (end <= at).astype(jnp.int32)
         first = jnp.where(end <= at, end, first)
     return doc, first
@@ -115,7 +115,7 @@
     def one(i, _):
         m, h, t = i // 52, (i // 26) % 2, i % 26
         r = jnp.maximum(t - 20, 0)
-        named = randoms[m, 0, 4 * s + 2 * h + r // 3, r % 3]
+        named = randoms[0, m, 4 * s + 2 * h + r // 3, r % 3]
         block = jnp.where(t < 18, 4 * s + 2 * h - 8 + t, named)
         inside = (block >= 0) & (block < 32)
         doc, first = doc_of(lengths, m, jnp.clip(block, 0, 31))
@@ -138,14 +138,14 @@
 
 def rest_block(lengths, randoms, s, m, t):
     r = jnp.maximum(t - 4, 0)
-    named = randoms[m, 0, 4 * s + r // 3, r % 3]
+    named = randoms[0, m, 4 * s + r // 3, r % 3]
     _, first = doc_of(lengths, m, 4 * s + 2 * jnp.minimum(t // 2, 1))
     return jnp.where(t < 4, first // 64 + t % 2, named)
 
 
-def forward_kernel(lengths, randoms, x_ref, wq, wk, wv, wo, wu, wd, vectors, b_up,
-                   att, lse, q_out, xs_out, k_out, v_out, wall, top_out, bias, extra, targets,
-                   own, mate, merged, merged_b, xall0, xall1, xs, ks, vs, wa,
+def forward_kernel(lengths, randoms, x_ref, wq_in, wk_in, wv_in, wo_in, wu_in, wd_in, v0, v1, v2, v3, v4, v5, v6, v7, b_up,
+                   att_out, lse, q_end, xs_out, k_out, v_out, wall, top_out, bias, extra_out, targets,
+                   wq, wk, wv, wo, wu, wd, att, q_out, extra, raw_sem, end_sem, own, mate, merged, merged_b, xall0, xall1, xs, ks, vs, wa,
                    mate_sem, lsem, osem, asend, arecv, acrecv, bsend, brecv, bcrecv, xsend, xrecv):
     z, x, y, c = place()
     s = 2 * z + x
@@ -179,13 +179,17 @@
         return remote(ref if src is None else src, ref, bsend.at[i, way],
                       bcrecv.at[i] if way == CC else brecv.at[i], to[way])
 
+    raw = [pltpu.make_async_copy(src, dst, raw_sem.at[i]) for i, (src, dst) in enumerate(
+        zip((wq_in, wk_in, wv_in, wo_in, wu_in, wd_in), (wq, wk, wv, wo, wu, wd)))]
+    for cp in raw:
+        cp.start()
     greet(z, x, y, c)
     for way in (UP, DOWN, XX):
         guarded(way, lambda way=way: x_copy(0, z, x, way, True).start())
     for m in range(2):
         pltpu.make_async_copy(x_ref.at[m], xall[m].at[pl.ds(4 * s, 4)], lsem.at[m]).start()
     owner = 4 * s + 2 * y + c
-    small = vectors[...].astype(F32)
+    small = jnp.concatenate([v[...].astype(F32) for v in (v0, v1, v2, v3, v4, v5, v6, v7)], axis=0)
     n = small.shape[1]
     own[0:8, :] = pltpu.roll(jnp.concatenate([small, jnp.zeros((8, 768 - n), F32)], axis=1), owner * n, axis=1)
     ups = b_up[...].astype(F32)
@@ -194,6 +198,8 @@
     ups = pltpu.roll(jnp.broadcast_to(ups, (8, 768)), (owner % 8) * n, axis=1)
     row = lax.broadcasted_iota(jnp.int32, (8, 768), 0)
     own[8:16, :] = jnp.where(row == owner // 8, ups, 0.0)
+    for cp in raw:
+        cp.wait()
     for i, ref in enumerate((wq, wk, wv, wo)):
         own[16 + 24 * i:40 + 24 * i, :] = ref[...].astype(F32)
     for j in range(4):
@@ -220,6 +226,8 @@
     keep_b = pltpu.make_async_copy(merged_b, wall.at[s * 2 + y, :, mine], lsem.at[3])
     keep_b.start()
     write_extra(lengths, randoms, s, extra)
+    extra_copy = pltpu.make_async_copy(extra, extra_out, end_sem.at[0])
+    extra_copy.start()
 
     lane = lax.broadcasted_iota(jnp.int32, (1, 1024), 1)
     for m in range(2):
@@ -358,6 +366,12 @@
 
         at_distance(arrived_x, k)
 
+    def q_copy(m):
+        return pltpu.make_async_copy(q_out.at[m], q_end.at[m], end_sem.at[1 + m])
+
+    def att_copy(m):
+        return pltpu.make_async_copy(att.at[m], att_out.at[m], end_sem.at[3 + m])
+
     def gather_near(m):
         x_here(m, 0)
         x_here(m, 1)
@@ -367,6 +381,7 @@
             xs[m, 256 * t:256 * t + 256, :] = chunk.reshape(256, chunk.shape[-1])
         q = (dot(xs[m, 512:768, :], wa[:, 16:64, :].reshape(768, 768)) + bias[0:1, :]).astype(BF)
         q_out[m] = q * jnp.asarray(0.125, BF)
+        q_copy(m).start()
 
     def gather_rest(m):
         x_here(m, 2)
@@ -430,6 +445,7 @@
             out_copy(m, 2).start()
 
         pl.when(i >= 3)(lambda: pair(m, i - 3))
+        pl.when(i == 8)(lambda: att_copy(m).start())
         pump(g)
         return 0
 
@@ -445,7 +461,10 @@
     lax.fori_loop(0, 16, b_arrived, 0)
     keep_b.wait()
     top_copy.wait()
+    extra_copy.wait()
     for m in range(2):
+        q_copy(m).wait()
+        att_copy(m).wait()
         for t in range(3):
             out_copy(m, t).wait()
 
@@ -526,9 +545,11 @@
             sd((16, REST, width), BF), sd((16, TOP, width), BF), sd((16, width), F32),
             sd((mb, 2, NK, 128), BF), sd((mb, 1, 1024), jnp.int32),
         ],
-        in_specs=[sm, sm, anywhere] + [vm] * 8,
-        out_specs=[vm, vm, vm, anywhere, anywhere, anywhere, anywhere, anywhere, vm, vm, vm],
+        in_specs=[sm, sm] + [anywhere] * 7 + [vm] * 9,
+        out_specs=[anywhere, vm] + [anywhere] * 6 + [vm, anywhere, vm],
         scratch_shapes=[
+            *[v(w.shape, BF) for w in weights], v((mb, rows, width), BF), v((mb, rows, width), BF),
+            v((mb, 2, NK, 128), BF), dma((6,)), dma((5,)),
             v((304, width), F32), v((304, 384), F32), v((TOP, 384), BF), v((REST, 384), BF),
             v((8 * rows // 64, 64, width), BF), v((8 * rows // 64, 64, width), BF),
             v((mb, NS, width), BF), v((mb, NS, width), BF), v((mb, NS, width), BF),
@@ -540,7 +561,7 @@
         compiler_params=pltpu.CompilerParams(
             collective_id=0, has_side_effects=True, vmem_limit_bytes=60 * 2**20
         ),
-    )(lengths, randoms, x.reshape(mb, rows // 64, 64, width), *weights, vectors, b_up)
+    )(lengths, randoms, x.reshape(mb, rows // 64, 64, width), *weights, *vectors, b_up)
 
 
 def backward_kernel(datt, stats, tgt, gb_in, extra_in, q_in, done, k_in, v_in, xs_in, top_in, go, gu, gd,
@@ -1010,21 +1031,21 @@
         cp.wait_send()
 
 
-STEP_ORDER = ("X", "TY", "W", "D1", "BF", "Y", "D0", "TX", "TZ", "D0F", "Z")
+STEP_ORDER = ("Y", "BF", "W", "TY", "TX", "Z", "X", "D0F", "D1", "TZ", "D0")
 STEPS = {
-    "Y": ((1, 1), (2, 2), (3, 3), (5, 4), (7, 5), (9, 6), (24, 7),),
-    "X": ((2, 0), (3, 1), (5, 2), (8, 3),),
-    "Z": ((11, 0), (12, 1), (20, 2),),
+    "Y": ((0, 1), (4, 2), (5, 3), (6, 4), (7, 5), (9, 6), (17, 7),),
+    "X": ((3, 0), (5, 1), (7, 2), (13, 3),),
+    "Z": ((12, 0), (16, 1), (19, 2),),
     "D0": ((14, 0), (18, 1), (23, 2),),
-    "TY": ((29, 0),),
-    "BF": ((29, 0),),
-    "W": ((32, 0),),
-    "D0F": ((24, 0),),
-    "TX": ((32, 0), (33, 1), (35, 2), (37, 3),),
-    "D1": ((27, 0), (29, 1), (32, 2),),
-    "TZ": ((33, 0), (35, 1), (37, 2),),
+    "TY": ((24, 0),),
+    "BF": ((27, 0),),
+    "W": ((27, 0),),
+    "D0F": ((32, 0),),
+    "TX": ((27, 0), (29, 1), (33, 2), (37, 3),),
+    "D1": ((25, 0), (28, 1), (29, 2),),
+    "TZ": ((31, 0), (33, 1), (37, 2),),
 }
-MATE_AT = 2
+MATE_AT = 3
 
 
 def backward_all(datt, stats, tgt, gb, extra, q, done, k, v, xs, top, go, gu, gd):
@@ -1130,18 +1151,32 @@
                       - normed * jnp.mean(c * normed, axis=-1, keepdims=True))
 
 
-def middle_kernel(att, x, cot, wall, bias, lse, out_ref, stats_ref, datt_ref, done_ref, go_out, gu_out, gd_out, gb_ref,
-                  go_ref, gu_ref, gd_ref, gsem, w, wsem, pre, hid, mid, low, n1, r1, ffn):
-    rows = x.shape[0]
-    copies = [
-        pltpu.make_async_copy(wall.at[:, pl.ds(0, 48), :], w.at[:, pl.ds(0, 48), :], wsem.at[0]),
-        pltpu.make_async_copy(wall.at[:, pl.ds(48, 192), :], w.at[:, pl.ds(48, 192), :], wsem.at[1]),
-        pltpu.make_async_copy(wall.at[:, pl.ds(240, 192), :], w.at[:, pl.ds(240, 192), :], wsem.at[2]),
-    ]
-    for cp in copies:
-        cp.start()
+def middle_kernel(att, x_in, cot_in, wall, bias, lse_in, out_ref, stats_ref, datt_ref, done_ref, go_out, gu_out, gd_out, gb_ref,
+                  x, cot, lse, isem, go_ref, gu_ref, gd_ref, gsem, w, wsem, pre, hid, mid, low, n1, r1, ffn):
+    rows = att.shape[0]
+    def load(j, t):
+        if t == 0:
+            src, dst = wall.at[:, pl.ds(0, 48), :], w.at[:, pl.ds(0, 48), :]
+        elif t == 1:
+            at = pl.ds(pl.multiple_of(48 + 48 * j, 16), 48)
+            src, dst = wall.at[:, at, :], w.at[:, at, :]
+        else:
+            at = pl.ds(4 * j, 4)
+            src, dst = wall.at[at, pl.ds(240, 192), :], w.at[at, pl.ds(240, 192), :]
+        return pltpu.make_async_copy(src, dst, wsem.at[t, j])
+
+    inputs = [pltpu.make_async_copy(src, dst, isem.at[i])
+              for i, (src, dst) in enumerate(((x_in, x), (cot_in, cot), (lse_in, lse)))]
+    load(0, 0).start()
+    inputs[0].start()
+    for j in range(4):
+        load(j, 1).start()
+        load(j, 2).start()
+    inputs[1].start()
+    inputs[2].start()
     half = rows // 2
-    copies[0].wait()
+    load(0, 0).wait()
+    inputs[0].wait()
     w_out = w[:, 0:48, :].reshape(768, 768)
     for h in range(2):
         r = pl.ds(h * half, half)
@@ -1153,8 +1188,6 @@
         mid[r, :] = value
         low[r, :] = value.astype(BF)
     ffn[...] = jnp.broadcast_to(bias[3:4, :], ffn.shape)
-    copies[1].wait()
-    copies[2].wait()
 
     def up_block(j):
         return w[:, pl.ds(pl.multiple_of(48 + 48 * j, 16), 48), :].reshape(768, 768)
@@ -1163,6 +1196,8 @@
         return w[pl.ds(4 * j, 4), 240:432, :].reshape(768, 768)
 
     def forward(j, _):
+        load(j, 1).wait()
+        load(j, 2).wait()
         wu, wd = up_block(j), down_block(j)
         for h in range(2):
             r = pl.ds(h * half, half)
@@ -1178,6 +1213,8 @@
 
     lax.fori_loop(0, 4, forward, 0)
     gb_ref[...] = jnp.zeros_like(gb_ref)
+    inputs[1].wait()
+    inputs[2].wait()
     for h in range(2):
         r = pl.ds(h * half, half)
         normed, inverse = norm(mid[r, :] + ffn[r, :])
@@ -1232,7 +1269,7 @@
             stats = jnp.where(lane == 17 + 2 * p, jnp.sum(jnp.where(lane >= 64, two, 0.0), axis=1, keepdims=True), stats)
         stats_ref[r, :] = stats
     go_ref[...] = dot_tn(att[...], low[...]).astype(BF)
-    go_copy = pltpu.make_async_copy(go_ref, go_out, wsem.at[0])
+    go_copy = pltpu.make_async_copy(go_ref, go_out, isem.at[3])
     go_copy.start()
     for j in range(4):
         sent(gd_ref, gd_out, j, 0).wait()
@@ -1241,19 +1278,21 @@
 
 
 def middle(att, x, cot, wall, bias, lse):
-    rows = x.shape[0]
+    rows = att.shape[0]
     sd = jax.ShapeDtypeStruct
-    vm = pl.BlockSpec(memory_space=pltpu.VMEM)
+    vm, anywhere = pl.BlockSpec(memory_space=pltpu.VMEM), pl.BlockSpec(memory_space=pl.ANY)
     return pl.pallas_call(
         middle_kernel,
-        in_specs=[vm, vm, vm, pl.BlockSpec(memory_space=pl.ANY), vm, vm],
+        in_specs=[vm, anywhere, anywhere, anywhere, vm, anywhere],
         out_specs=[vm] * 4 + [pl.BlockSpec(memory_space=pl.ANY)] * 3 + [vm],
         out_shape=[sd((rows, 768), BF), sd((rows, 128), F32), sd((rows, 768), BF), sd((rows, 768), F32), sd((768, 768), BF),
                    sd((768, 3072), BF), sd((3072, 768), BF), sd((16, 768), F32)],
         scratch_shapes=[
+            pltpu.VMEM((rows, 768), BF), pltpu.VMEM((rows, 768), BF), pltpu.VMEM((rows, 128), F32),
+            pltpu.SemaphoreType.DMA((4,)),
             pltpu.VMEM((768, 768), BF), pltpu.VMEM((4, 768, 768), BF), pltpu.VMEM((4, 768, 768), BF),
             pltpu.SemaphoreType.DMA((2, 4)),
-            pltpu.VMEM((16, 432, 768), BF), pltpu.SemaphoreType.DMA((3,)),
+            pltpu.VMEM((16, 432, 768), BF), pltpu.SemaphoreType.DMA((3, 4)),
             pltpu.VMEM((4, rows, 768), F32), pltpu.VMEM((4, rows, 768), BF),
             pltpu.VMEM((rows, 768), F32), pltpu.VMEM((rows, 768), BF), pltpu.VMEM((rows, 768), F32),
             pltpu.VMEM((rows, 128), F32), pltpu.VMEM((rows, 768), F32),
@@ -1523,7 +1562,8 @@
     flat = lambda t: t.reshape(-1, t.shape[-1])
     if linked:
         att, lse, q, xs, k, v, wall, top, bias, extra, targets = forward_all(
-            doc_lengths, random_blocks, x, (wq, wk, wv, wo, wu, wd), jnp.stack(vectors), b_up[None])
+            doc_lengths.transpose(1, 0, 2), random_blocks.transpose(1, 0, 2, 3), x, (wq, wk, wv, wo, wu, wd),
+            [v[None] for v in vectors], b_up[None])
     else:
         where, see = block_plan(lengths, randoms, device, seq_len // BLK)
         extra, table = mask_columns(see), vector_table(vectors, b_up, owner, width)

time: 311 us -> 303 us (0.974)
  Pallas kernels: 307 us -> 301 us
    pallas_call x1, Pallas kernels: 148 us -> 142 us  [backward_all(): pl.pallas_call(backward_kernel, out_shape=[sd((24, width), F32)] * 4 + [s...]
where the time goes in v2:
time: 303 us
  Pallas kernels  301 us (99%)
    pallas_call x1, Pallas kernels, backward_all(): pl.pallas_call(backward_kernel, out_shape=[sd((24, width), F32)] * 4 + [s...  142 us
    pallas_call x1, Pallas kernels, forward_all(): pl.pallas_call(forward_kernel, out_shape=[sd((mb, rows, width), BF), sd((...  124 us
    pallas_call x1, Pallas kernels, middle(): pl.pallas_call(middle_kernel, in_specs=[vm, anywhere, anywhere, anywhere,...  31.7 us

profile of v2, /device:TPU:0, one launch (start us, length us, event | category | flops | bytes accessed | tf_op | source)
XLA Modules:
  0.0 302.9 jit_solution(13661463237077236963)
XLA Ops:
  0.7 1.4 copy.36
  2.0 123.7 %shard_map.314 = (bf16[2,256,768]{2,1,0:T(8,128)(2,1)}, f32[2,256,128]{2,1,0:T(8,128)}, bf16[2,256,768]{2,1,0:T(8,128)(2,1)}, bf16[2,2304,768]{2,1,0:T(8,128)(2,...) custom-call(s32[1,2,4]{2,1,0:T(2,128)} %bitcast.51, ...), custom_call_target="tpu_custom_call" | custom-call | tf_op jit(solution)/shard_map/pallas_call | solution.py:540
  125.7 31.7 %shard_map.315 = (bf16[512,768]{1,0:T(8,128)(2,1)}, f32[512,128]{1,0:T(8,128)}, bf16[512,768]{1,0:T(8,128)(2,1)}, f32[512,768]{1,0:T(8,128)}, bf16[768,768]{1,0:...) custom-call(bf16[512,768]{1,0:T(8,128)(2,1)} %bitcast.46, ...), custom_call_target="tpu_custom_call" | custom-call | tf_op jit(solution)/shard_map/pallas_call | solution.py:1284
  157.4 142.0 %shard_map.316 = (f32[24,768]{1,0:T(8,128)}, f32[24,768]{1,0:T(8,128)}, f32[24,768]{1,0:T(8,128)}, f32[24,768]{1,0:T(8,128)}, f32[24,3072]{1,0:T(8,128)}, /*inde...) custom-call(bf16[2,256,768]{2,1,0:T(8,128)(2,1)} %bitcast.47, f32[2,256,128]{2,1,0:T(8,128)} %bitcast.48, ...), custom_call_target="tpu_custom_call" | custom-call | tf_op jit(solution)/shard_map/pallas_call | solution.py:1059
  299.4 3.3 %shard_map.317 = (f32[24,768]{1,0:T(8,128)}, f32[24,768]{1,0:T(8,128)}, f32[24,768]{1,0:T(8,128)}, f32[24,768]{1,0:T(8,128)}, f32[24,3072]{1,0:T(8,128)}, /*inde...) custom-call(f32[16,768]{1,0:T(8,128)} %get-tuple-element.79.refs_0_,, ...), custom_call_target="tpu_custom_call" | custom-call | tf_op jit(solution)/shard_map/pallas_call | solution.py:1407

commit v3 on v2

--- a/solution.py
+++ b/solution.py
@@ -1174,11 +1174,11 @@
         load(j, 2).start()
     inputs[1].start()
     inputs[2].start()
-    half = rows // 2
+    half = rows
     load(0, 0).wait()
     inputs[0].wait()
     w_out = w[:, 0:48, :].reshape(768, 768)
-    for h in range(2):
+    for h in range(1):
         r = pl.ds(h * half, half)
         t = x[r, :].astype(F32) + dot(att[r, :], w_out) + bias[2:3, :]
         normed, inverse = norm(t)
@@ -1199,7 +1199,7 @@
         load(j, 1).wait()
         load(j, 2).wait()
         wu, wd = up_block(j), down_block(j)
-        for h in range(2):
+        for h in range(1):
             r = pl.ds(h * half, half)
             u = dot(low[r, :], wu) + bias[pl.ds(8 + j, 1), :]
             square = u * u
@@ -1215,7 +1215,7 @@
     gb_ref[...] = jnp.zeros_like(gb_ref)
     inputs[1].wait()
     inputs[2].wait()
-    for h in range(2):
+    for h in range(1):
         r = pl.ds(h * half, half)
         normed, inverse = norm(mid[r, :] + ffn[r, :])
         out_ref[r, :] = (normed * bias[6:7, :] + bias[7:8, :]).astype(BF)
@@ -1237,7 +1237,7 @@
         d_ffn = datt_ref[...]
         gd_ref[j] = dot_tn(hid[j], d_ffn).astype(BF)
         sent(gd_ref, gd_out, j, 0).start()
-        for h in range(2):
+        for h in range(1):
             r = pl.ds(h * half, half)
             d_pre = (dot_nt(datt_ref[r, :], wd) * pre[j, r, :]).astype(BF)
             hid[j, r, :] = d_pre
@@ -1248,7 +1248,7 @@
         return 0
 
     lax.fori_loop(0, 4, backward, 0)
-    for h in range(2):
+    for h in range(1):
         r = pl.ds(h * half, half)
         d_mid, normed = mid[r, :], n1[r, :]
         gb_ref[4:5, :] += jnp.sum(d_mid * normed, axis=0, keepdims=True)

time: 303 us -> 303 us (level)
  no operation moved by 1% of the time
where the time goes in v3:
time: 303 us; the launch traced here: 302 us
  Pallas kernels  300 us (99%)
    pallas_call x1, Pallas kernels, backward_all(): pl.pallas_call(backward_kernel, out_shape=[sd((24, width), F32)] * 4 + [s...  142 us
    pallas_call x1, Pallas kernels, forward_all(): pl.pallas_call(forward_kernel, out_shape=[sd((mb, rows, width), BF), sd((...  124 us
    pallas_call x1, Pallas kernels, middle(): pl.pallas_call(middle_kernel, in_specs=[vm, anywhere, anywhere, anywhere,...  31.3 us

profile of v3, /device:TPU:0, one launch (start us, length us, event | category | flops | bytes accessed | tf_op | source)
XLA Modules:
  0.0 302.5 jit_solution(3945213087179548404)
XLA Ops:
  0.7 1.4 copy.36
  2.0 123.7 %shard_map.314 = (bf16[2,256,768]{2,1,0:T(8,128)(2,1)}, f32[2,256,128]{2,1,0:T(8,128)}, bf16[2,256,768]{2,1,0:T(8,128)(2,1)}, bf16[2,2304,768]{2,1,0:T(8,128)(2,...) custom-call(s32[1,2,4]{2,1,0:T(2,128)} %bitcast.51, ...), custom_call_target="tpu_custom_call" | custom-call | tf_op jit(solution)/shard_map/pallas_call | solution.py:540
  125.7 31.3 %shard_map.315 = (bf16[512,768]{1,0:T(8,128)(2,1)}, f32[512,128]{1,0:T(8,128)}, bf16[512,768]{1,0:T(8,128)(2,1)}, f32[512,768]{1,0:T(8,128)}, bf16[768,768]{1,0:...) custom-call(bf16[512,768]{1,0:T(8,128)(2,1)} %bitcast.46, ...), custom_call_target="tpu_custom_call" | custom-call | tf_op jit(solution)/shard_map/pallas_call | solution.py:1284
  157.0 142.0 %shard_map.316 = (f32[24,768]{1,0:T(8,128)}, f32[24,768]{1,0:T(8,128)}, f32[24,768]{1,0:T(8,128)}, f32[24,768]{1,0:T(8,128)}, f32[24,3072]{1,0:T(8,128)}, /*inde...) custom-call(bf16[2,256,768]{2,1,0:T(8,128)(2,1)} %bitcast.47, f32[2,256,128]{2,1,0:T(8,128)} %bitcast.48, ...), custom_call_target="tpu_custom_call" | custom-call | tf_op jit(solution)/shard_map/pallas_call | solution.py:1059
  299.0 3.3 %shard_map.317 = (f32[24,768]{1,0:T(8,128)}, f32[24,768]{1,0:T(8,128)}, f32[24,768]{1,0:T(8,128)}, f32[24,768]{1,0:T(8,128)}, f32[24,3072]{1,0:T(8,128)}, /*inde...) custom-call(f32[16,768]{1,0:T(8,128)} %get-tuple-element.79.refs_0_,, ...), custom_call_target="tpu_custom_call" | custom-call | tf_op jit(solution)/shard_map/pallas_call | solution.py:1407
